TPU v7x, 32 devices: a whole 2x2x4 slice. The times are simulated.
32 devices in a mesh: shot: 8 (over z, y), freq: 4 (over x, core).
Axes of the slice: x: 2, y: 2, z: 4, core: 2. Of those that a mesh axis runs over, the one named last changes fastest.
Arguments:
- blended: bfloat16 [2, 32, 512, 256], P(None, 'shot', 'freq'), may hold values from -6 to 6
- estimate: bfloat16 [2, 32, 512, 256], P(None, 'shot', 'freq'), may hold values from -5 to 5
- partner: int32 [32], P('shot'), may hold values from 0 to 31, as said below
- delays: int32 [32], replicated, may hold values from 0 to 256
- levels: int32 [8], replicated, may hold values from 1 to 4
Outputs:
- deblended: bfloat16 [2, 32, 512, 256], P(None, 'shot', 'freq')
Inputs may be any that keep to these rules, and one draw needn't show every extreme that they name: Shot s of block b = s // 4 is paired with a shot of block (b + 4) modulo 32 / 4; the pairing is mutual, partner[partner[s]] = s.
All inputs are finite; a program needn't handle non-finite values.
Results may differ from a plain program's by a relative error of at most 0.005.
Values may be sent and summed in bfloat16 or wider, within the bound.
A program may use at most 64 MiB of HBM per device.

v0:
```python
import functools
import math

import jax
import jax.numpy as jnp
import numpy as np
from jax import lax
from jax.experimental import pallas as pl
from jax.experimental.pallas import tpu as pltpu
from jax.sharding import PartitionSpec as P

NF = 512
NT = 1024
PASSES = 2


relaxation = 0.5
level_scale = 0.25


def tables(length):
    indices = jnp.arange(length, dtype=jnp.int32)
    products = jnp.mod(indices[:, None] * indices[None, :], length)
    angles = 2.0 * math.pi / length * products.astype(jnp.float32)
    return (jnp.cos(angles), jnp.sin(angles))


def spectrum(real_part, imag_part, direction_sign, shot_cos, shot_sin, recv_cos, recv_sin):
    highest = lax.Precision.HIGHEST

    def receivers(values, table):
        return jnp.einsum("...n,nk->...k", values, table, precision=highest)

    def shots(values, table):
        return jnp.einsum("tk,...tfn->...kfn", table, values, precision=highest)

    first_real = receivers(real_part, recv_cos) + direction_sign * receivers(imag_part, recv_sin)
    first_imag = receivers(imag_part, recv_cos) - direction_sign * receivers(real_part, recv_sin)
    out_real = shots(first_real, shot_cos) + direction_sign * shots(first_imag, shot_sin)
    out_imag = shots(first_imag, shot_cos) - direction_sign * shots(first_real, shot_sin)
    scale = 1.0 / math.sqrt(shot_cos.shape[0] * recv_cos.shape[0])
    return (out_real * scale, out_imag * scale)


def shrink(real_part, imag_part, threshold):
    modulus = jnp.sqrt(real_part * real_part + imag_part * imag_part)
    factor = jnp.maximum(modulus - threshold, 0.0) / jnp.maximum(modulus, threshold)
    return (real_part * factor, imag_part * factor)


def phase_tables(offsets, frequency):
    phase_index = jnp.mod(frequency[None, :] * offsets[:, None], NT)
    angles = 2.0 * math.pi / NT * phase_index.astype(jnp.float32)
    return (jnp.cos(angles)[:, :, None], jnp.sin(angles)[:, :, None])


def relax_step(current, blended, partner_recs, phase_cos, phase_sin):
    shifted_real = partner_recs[0] * phase_cos + partner_recs[1] * phase_sin
    shifted_imag = partner_recs[1] * phase_cos - partner_recs[0] * phase_sin
    shifted = jnp.stack([shifted_real, shifted_imag])
    current_f = current.astype(jnp.float32)
    return current_f + relaxation * (blended.astype(jnp.float32) - current_f - shifted)


def whole_pass(
    current, blended, partner_all, phase_cos, phase_sin, level_all, taper, tables_all, block
):
    shot_cos, shot_sin, recv_cos, recv_sin = tables_all
    total_shots = current.shape[1]
    few_freq = current.shape[2]
    receivers_count = current.shape[3]
    count = total_shots // block
    partner_recs = jnp.take(current, partner_all, axis=1).astype(jnp.float32)
    updated = relax_step(current, blended, partner_recs, phase_cos, phase_sin)
    grouped = jnp.transpose(
        updated.reshape(2, count, block, few_freq, receivers_count), (1, 0, 2, 3, 4)
    )
    following = jnp.concatenate([grouped[1:], jnp.zeros_like(grouped[:1])], axis=0)
    segments = jnp.concatenate([grouped, following], axis=2) * taper[None, None, :, None, None]
    coef_real, coef_imag = spectrum(
        segments[:, 0], segments[:, 1], 1.0, shot_cos, shot_sin, recv_cos, recv_sin
    )
    modulus = jnp.sqrt(coef_real * coef_real + coef_imag * coef_imag)
    local_sum = jnp.sum(modulus, axis=(1, 2, 3))
    total_sum = lax.psum(local_sum, ("shot", "freq"))
    span = 2 * block
    threshold = (level_scale * level_all * total_sum / (span * NF * receivers_count))[
        :, None, None, None
    ]
    kept_real, kept_imag = shrink(coef_real, coef_imag, threshold)
    back_real, back_imag = spectrum(
        kept_real, kept_imag, -1.0, shot_cos, shot_sin, recv_cos, recv_sin
    )
    result = jnp.stack([back_real, back_imag], axis=1)
    firsts = result[:, :, :block]
    seconds = jnp.concatenate(
        [jnp.zeros_like(result[:1, :, block:]), result[:-1, :, block:]], axis=0
    )
    summed = firsts + seconds
    return (
        jnp.transpose(summed, (1, 0, 2, 3, 4))
        .reshape(2, total_shots, few_freq, receivers_count)
        .astype(jnp.bfloat16)
    )


def on_device(blended, estimate, partner, delays, levels):
    block = estimate.shape[1]
    freq_local = estimate.shape[2]
    receivers_count = estimate.shape[3]
    span = 2 * block
    steps_t = jnp.arange(span, dtype=jnp.float32)
    taper = jnp.sin(math.pi * (steps_t + 0.5) / span) ** 2
    shot_cos, shot_sin = tables(span)
    recv_cos, recv_sin = tables(receivers_count)
    tables_all = (shot_cos, shot_sin, recv_cos, recv_sin)
    blended_all, current = (
        lax.all_to_all(blended, "shot", split_axis=2, concat_axis=1, tiled=True),
        lax.all_to_all(estimate, "shot", split_axis=2, concat_axis=1, tiled=True),
    )
    few_freq = current.shape[2]
    partner_all = lax.all_gather(partner, "shot", axis=0, tiled=True)
    offsets = jnp.take(delays, partner_all) - delays
    frequency = (
        lax.axis_index("freq") * freq_local
        + lax.axis_index("shot") * few_freq
        + jnp.arange(few_freq, dtype=jnp.int32)
    )
    phase_cos, phase_sin = phase_tables(offsets, frequency)
    level_all = levels.astype(jnp.float32)
    for pass_index in range(PASSES):
        current = whole_pass(
            current,
            blended_all,
            partner_all,
            phase_cos,
            phase_sin,
            level_all,
            taper,
            tables_all,
            block,
        )
    return lax.all_to_all(current, "shot", split_axis=1, concat_axis=2, tiled=True)


LANES = 128
TINY = 1.1754944e-38


def fourier_matrices(length):
    indices = np.arange(length)
    angles = 2.0 * np.pi / length * (np.outer(indices, indices) % length)
    cos, sin = np.cos(angles), np.sin(angles)
    forward = np.block([[cos, -sin], [sin, cos]])

    def split(matrix):
        hi = matrix.astype(jnp.bfloat16)
        lo = (matrix - hi.astype(np.float64)).astype(jnp.bfloat16)
        return np.stack([hi, lo])

    return split(forward), split(forward.T)


def short_fourier(values, sign):
    count = len(values)
    if count == 1:
        return values
    even = short_fourier(values[0::2], sign)
    odd = short_fourier(values[1::2], sign)
    low, high = [], []
    for k in range(count // 2):
        real, imag = odd[k]
        if 4 * k == count:
            real, imag = (-imag, real) if sign > 0 else (imag, -real)
        elif 8 * k == count or 8 * k == 3 * count:
            half = math.sqrt(0.5)
            turned = (real - sign * imag, imag + sign * real)
            if 8 * k == 3 * count:
                turned = (-real - sign * imag, sign * real - imag)
            real, imag = turned[0] * half, turned[1] * half
        elif k:
            cos = math.cos(2.0 * math.pi * k / count)
            sin = sign * math.sin(2.0 * math.pi * k / count)
            real, imag = real * cos - imag * sin, imag * cos + real * sin
        low.append((even[k][0] + real, even[k][1] + imag))
        high.append((even[k][0] - real, even[k][1] - imag))
    return low + high


def flipped(index, mask, count):
    result, bit = 0, 1
    while bit < count:
        result = result + (index // bit + mask // bit) % 2 * bit
        bit *= 2
    return result


def deblend_kernel(
    n,
    nf,
    block,
    few,
    nr,
    blended_ref,
    estimate_ref,
    partner_ref,
    delays_ref,
    levels_ref,
    forward_hbm,
    inverse_hbm,
    out_ref,
    e_all,
    b_all,
    info,
    turn_cos,
    turn_sin,
    turn_pick,
    x_hi,
    x_lo,
    lines,
    coefs,
    carry,
    limit,
    near_sums,
    far_sums,
    forward,
    inverse,
    local_sem,
    info_send,
    info_recv,
    e_send,
    e_recv,
    b_send,
    b_recv,
    near_send,
    near_recv,
    far_send,
    far_recv,
    out_send,
    out_recv,
):
    total = n * block
    span = 2 * block
    half = n // 2
    me = lax.axis_index("shot")
    column = lax.axis_index("freq")
    mesh_id = pl.DeviceIdType.MESH
    peers = [flipped(me, k, n) for k in range(n)]
    order = list(range(half, n)) + list(range(1, half))
    others = [lax.rem(column + k, nf) for k in range(nf)]

    barrier = pltpu.get_barrier_semaphore()
    for k in order:
        pl.semaphore_signal(barrier, inc=1, device_id={"shot": peers[k]}, device_id_type=mesh_id)
    for k in range(1, nf):
        pl.semaphore_signal(barrier, inc=1, device_id={"freq": others[k]}, device_id_type=mesh_id)

    local_copies = [
        pltpu.make_async_copy(forward_hbm, forward, local_sem.at[0]),
        pltpu.make_async_copy(inverse_hbm, inverse, local_sem.at[1]),
        pltpu.make_async_copy(
            estimate_ref.at[:, :, pl.ds(me * few, few), :],
            e_all.at[:, pl.ds(me * block, block)],
            local_sem.at[2],
        ),
        pltpu.make_async_copy(
            blended_ref.at[:, :, pl.ds(me * few, few), :],
            b_all.at[:, pl.ds(me * block, block)],
            local_sem.at[3],
        ),
    ]
    for copy in local_copies:
        copy.start()

    lane = lax.broadcasted_iota(jnp.int32, (8, LANES), 1)
    row = lax.broadcasted_iota(jnp.int32, (8, LANES), 0)
    tile = jnp.zeros((8, LANES), jnp.int32)
    for i in range(block):
        own = me * block + i
        mate = partner_ref[i]
        offset = delays_ref[mate] - delays_ref[own]
        here = lane == own
        tile = jnp.where(here & (row == 0), mate, tile)
        tile = jnp.where(here & (row == 1), offset, tile)
    info[0] = tile

    pl.semaphore_wait(barrier, n + nf - 2)

    def send(source, target, send_sem, recv_sem, where):
        copy = pltpu.make_async_remote_copy(
            src_ref=source,
            dst_ref=target,
            send_sem=send_sem,
            recv_sem=recv_sem,
            device_id=where,
            device_id_type=mesh_id,
        )
        copy.start()
        return copy

    info_copies = [
        send(info.at[0], info.at[k], info_send.at[k], info_recv.at[k], {"shot": peers[k]})
        for k in order
    ]
    record_copies = []
    for k in order:
        for held, whole, sent, received in (
            (estimate_ref, e_all, e_send, e_recv),
            (blended_ref, b_all, b_send, b_recv),
        ):
            record_copies.append(
                send(
                    held.at[:, :, pl.ds(peers[k] * few, few), :],
                    whole.at[:, pl.ds(me * block, block)],
                    sent.at[k],
                    received.at[k],
                    {"shot": peers[k]},
                )
            )

    lines[pl.ds(total, block)] = jnp.zeros((block, few, 2 * nr), jnp.float32)
    for copy in info_copies:
        copy.wait()
    known = info[0]
    for k in range(1, n):
        known = known + info[k]
    frequency = (column * n + me) * few + lax.broadcasted_iota(jnp.int32, (few, LANES), 0)
    phase = (frequency * known[1:2, :]) & (NT - 1)
    angles = 2.0 * math.pi / NT * phase.astype(jnp.float32)
    cos_table = relaxation * jnp.cos(angles)
    sin_table = relaxation * jnp.sin(angles)
    for s in range(total):
        first = (s // block + half) % n * block
        turn_cos[s] = jnp.broadcast_to(cos_table[:, s : s + 1], (few, LANES))
        turn_sin[s] = jnp.broadcast_to(sin_table[:, s : s + 1], (few, LANES))
        turn_pick[s] = jnp.broadcast_to(known[0:1, s : s + 1] - first, (few, LANES))

    for copy in record_copies:
        copy.wait()
    for copy in local_copies:
        copy.wait()

    def keep(s, lanes, value):
        top = value.astype(jnp.bfloat16)
        x_hi[s, :, lanes] = top
        x_lo[s, :, lanes] = (value - top.astype(jnp.float32)).astype(jnp.bfloat16)

    def relax(pair, carried):
        for c in range(0, nr, LANES):
            lanes = slice(c, c + LANES)
            records = [
                [
                    [
                        e_all[part, (pair + side * half) * block + i, :, lanes].astype(jnp.float32)
                        for part in range(2)
                    ]
                    for i in range(block)
                ]
                for side in range(2)
            ]
            for side in range(2):
                for i in range(block):
                    s = (pair + side * half) * block + i
                    pick = turn_pick[s]
                    cos, sin = turn_cos[s], turn_sin[s]
                    mate_real, mate_imag = records[1 - side][0]
                    for j in range(1, block):
                        mate_real = jnp.where(pick == j, records[1 - side][j][0], mate_real)
                        mate_imag = jnp.where(pick == j, records[1 - side][j][1], mate_imag)
                    real, imag = records[side][i]
                    seen_real = b_all[0, s, :, lanes].astype(jnp.float32)
                    seen_imag = b_all[1, s, :, lanes].astype(jnp.float32)
                    keep(
                        s,
                        lanes,
                        real + relaxation * (seen_real - real) - (mate_real * cos + mate_imag * sin),
                    )
                    keep(
                        s,
                        slice(nr + c, nr + c + LANES),
                        imag + relaxation * (seen_imag - imag) - (mate_imag * cos - mate_real * sin),
                    )
        return carried

    def receivers(start, table):
        rows = (total // 2) * few
        top = x_hi[pl.ds(start, total // 2)].reshape(rows, 2 * nr)
        rest = x_lo[pl.ds(start, total // 2)].reshape(rows, 2 * nr)
        result = jnp.dot(top, table[0], preferred_element_type=jnp.float32)
        result = result + jnp.dot(rest, table[0], preferred_element_type=jnp.float32)
        result = result + jnp.dot(top, table[1], preferred_element_type=jnp.float32)
        return result.reshape(total // 2, few, 2 * nr)

    weights = [math.sin(math.pi * (t + 0.5) / span) ** 2 for t in range(span)]

    def analyse(step):
        def window(j, carried):
            summed = jnp.zeros((few, LANES), jnp.float32)
            for c in range(0, nr, LANES):
                values = [
                    (
                        lines[j * block + t, :, c : c + LANES] * weights[t],
                        lines[j * block + t, :, nr + c : nr + c + LANES] * weights[t],
                    )
                    for t in range(span)
                ]
                for k, (real, imag) in enumerate(short_fourier(values, -1)):
                    power = real * real + imag * imag
                    summed = summed + power * lax.rsqrt(jnp.maximum(power, TINY))
                    coefs[j, k, :, c : c + LANES] = real
                    coefs[j, k, :, nr + c : nr + c + LANES] = imag
            near_sums[step, 0, pl.ds(j, 1), :] = jnp.sum(summed, axis=0, keepdims=True)
            return carried

        lax.fori_loop(0, n, window, 0)

    def thresholds(step):
        copies = [
            send(
                near_sums.at[step, 0],
                near_sums.at[step, k],
                near_send.at[step, k],
                near_recv.at[step, k],
                {"shot": peers[k]},
            )
            for k in order
        ]
        for copy in copies:
            copy.wait()
        part = near_sums[step, 0]
        for k in range(1, n):
            part = part + near_sums[step, k]
        far_sums[step, 0] = part
        copies = [
            send(
                far_sums.at[step, 0],
                far_sums.at[step, k],
                far_send.at[step, k],
                far_recv.at[step, k],
                {"freq": others[k]},
            )
            for k in range(1, nf)
        ]
        for copy in copies:
            copy.wait()
        for k in range(1, nf):
            part = part + far_sums[step, k]
        limit[...] = jnp.broadcast_to(jnp.sum(part, axis=1, keepdims=True), (n, LANES))

    scale = 1.0 / (span * nr)
    count = span * few * n * nf * nr

    def synthesise(j, carried):
        level = levels_ref[j].astype(jnp.float32) * (level_scale * scale / count)
        bound = limit[pl.ds(j, 1), :] * level
        for c in range(0, nr, LANES):
            values = []
            for k in range(span):
                real = coefs[j, k, :, c : c + LANES]
                imag = coefs[j, k, :, nr + c : nr + c + LANES]
                power = real * real + imag * imag
                factor = jnp.maximum(scale - bound * lax.rsqrt(power), 0.0)
                values.append((real * factor, imag * factor))
            for t, parts in enumerate(short_fourier(values, 1)):
                for part in range(2):
                    lanes = slice(part * nr + c, part * nr + c + LANES)
                    if t < block:
                        keep(j * block + t, lanes, parts[part] + carry[t, :, lanes])
                    else:
                        carry[t - block, :, lanes] = parts[part]
        return carried

    for step in range(PASSES):
        lax.fori_loop(0, half, relax, 0)
        for start in (0, total // 2):
            lines[pl.ds(start, total // 2)] = receivers(start, forward)
        analyse(step)
        thresholds(step)
        carry[...] = jnp.zeros_like(carry)
        lax.fori_loop(0, n, synthesise, 0)
        if step < PASSES - 1:
            for start in (0, total // 2):
                result = receivers(start, inverse).astype(jnp.bfloat16)
                e_all[0, pl.ds(start, total // 2)] = result[:, :, :nr]
                e_all[1, pl.ds(start, total // 2)] = result[:, :, nr:]

    copies = []
    mine = me // half
    for side, group in ((1 - mine, range(half, n)), (mine, range(1, half))):
        start = side * (total // 2)
        result = receivers(start, inverse).astype(jnp.bfloat16)
        e_all[0, pl.ds(start, total // 2)] = result[:, :, :nr]
        e_all[1, pl.ds(start, total // 2)] = result[:, :, nr:]
        for k in group:
            copies.append(
                send(
                    e_all.at[:, pl.ds(peers[k] * block, block)],
                    out_ref.at[:, :, pl.ds(me * few, few), :],
                    out_send.at[k],
                    out_recv.at[k],
                    {"shot": peers[k]},
                )
            )
    last = pltpu.make_async_copy(
        e_all.at[:, pl.ds(me * block, block)],
        out_ref.at[:, :, pl.ds(me * few, few), :],
        local_sem.at[0],
    )
    last.start()
    for copy in copies:
        copy.wait()
    last.wait()


def in_one_kernel(n, nf, blended, estimate, partner, delays, levels):
    block, freq_local, nr = estimate.shape[1:]
    few = freq_local // n
    total = n * block
    forward, inverse = fourier_matrices(nr)
    f32, bf16 = jnp.float32, jnp.bfloat16
    anywhere = pl.BlockSpec(memory_space=pl.ANY)
    scalars = pl.BlockSpec(memory_space=pltpu.SMEM)
    dma = pltpu.SemaphoreType.DMA
    return pl.pallas_call(
        functools.partial(deblend_kernel, n, nf, block, few, nr),
        out_shape=jax.ShapeDtypeStruct(estimate.shape, estimate.dtype),
        in_specs=[anywhere, anywhere, scalars, scalars, scalars, anywhere, anywhere],
        out_specs=anywhere,
        scratch_shapes=[
            pltpu.VMEM((2, total, few, nr), bf16),
            pltpu.VMEM((2, total, few, nr), bf16),
            pltpu.VMEM((n, 8, LANES), jnp.int32),
            pltpu.VMEM((total, few, LANES), f32),
            pltpu.VMEM((total, few, LANES), f32),
            pltpu.VMEM((total, few, LANES), jnp.int32),
            pltpu.VMEM((total, few, 2 * nr), bf16),
            pltpu.VMEM((total, few, 2 * nr), bf16),
            pltpu.VMEM((total + block, few, 2 * nr), f32),
            pltpu.VMEM((n, 2 * block, few, 2 * nr), f32),
            pltpu.VMEM((block, few, 2 * nr), f32),
            pltpu.VMEM((n, LANES), f32),
            pltpu.VMEM((PASSES, n, n, LANES), f32),
            pltpu.VMEM((PASSES, nf, n, LANES), f32),
            pltpu.VMEM(forward.shape, bf16),
            pltpu.VMEM(inverse.shape, bf16),
            dma((4,)),
            dma((n,)),
            dma((n,)),
            dma((n,)),
            dma((n,)),
            dma((n,)),
            dma((n,)),
            dma((PASSES, n)),
            dma((PASSES, n)),
            dma((PASSES, nf)),
            dma((PASSES, nf)),
            dma((n,)),
            dma((n,)),
        ],
        compiler_params=pltpu.CompilerParams(
            collective_id=0, has_side_effects=True, vmem_limit_bytes=48 * 1024 * 1024
        ),
    )(blended, estimate, partner, delays, levels, jnp.asarray(forward), jnp.asarray(inverse))


def solution(mesh):
    n, nf = mesh.shape["shot"], mesh.shape["freq"]

    def body(blended, estimate, partner, delays, levels):
        block, freq_local, nr = estimate.shape[1:]
        whole_tiles = (
            n == 8 and freq_local % (16 * n) == 0 and nr % LANES == 0 and n * block <= LANES
        )
        if whole_tiles:
            return in_one_kernel(n, nf, blended, estimate, partner, delays, levels)
        return on_device(blended, estimate, partner, delays, levels)

    return jax.shard_map(
        body,
        mesh=mesh,
        in_specs=(
            P(None, "shot", "freq", None),
            P(None, "shot", "freq", None),
            P("shot"),
            P(),
            P(),
        ),
        out_specs=P(None, "shot", "freq", None),
        check_vma=False,
    )
```

profile of v0, /device:TPU:0, one launch (start us, length us, event | category | flops | bytes accessed | tf_op | source)
XLA Modules:
  0.0 71.9 jit_solution(17213654061935263750)
XLA Ops:
  0.0 0.0 copy-start
  0.0 1.2 %copy-done = bf16[2,512,512]{2,1,0:T(8,128)(2,1)S(1)} copy-done((bf16[2,512,512]{2,1,0:T(8,128)(2,1)S(1)}, bf16[2,512,512]{2,1,0:T(8,128)(2,1)}, u32[]{:S(2)}) %copy-start) | copy-done | bytes 1048600
  1.2 0.0 copy-start.1
  1.2 1.2 %copy-done.1 = bf16[2,512,512]{2,1,0:T(8,128)(2,1)S(1)} copy-done((bf16[2,512,512]{2,1,0:T(8,128)(2,1)S(1)}, bf16[2,512,512]{2,1,0:T(8,128)(2,1)}, u32[]{:S(2)}) %copy-start.1) | copy-done | bytes 1048600
  2.5 0.0 copy-start.2
  2.5 1.0 %copy-done.2 = bf16[2,4,128,256]{3,2,1,0:T(8,128)(2,1)S(1)} copy-done((bf16[2,4,128,256]{3,2,1,0:T(8,128)(2,1)S(1)}, bf16[2,4,128,256]{3,2,1,0:T(8,128)(2,1)}, u32[]{:S(2)}) %copy-start.2) | copy-done | bytes 524312
  3.5 0.0 copy-start.3
  3.5 1.0 %copy-done.3 = bf16[2,4,128,256]{3,2,1,0:T(8,128)(2,1)S(1)} copy-done((bf16[2,4,128,256]{3,2,1,0:T(8,128)(2,1)S(1)}, bf16[2,4,128,256]{3,2,1,0:T(8,128)(2,1)}, u32[]{:S(2)}) %copy-start.3) | copy-done | bytes 524312
  4.5 0.0 copy-start.4
  4.5 0.7 copy-done.4
  5.2 0.0 copy-start.5
  5.2 0.7 copy-done.5
  5.8 0.0 copy-start.6
  5.8 0.7 copy-done.6
  6.5 64.5 %shard_map.73 = bf16[2,4,128,256]{3,2,1,0:T(8,128)(2,1)S(1)} custom-call(bf16[2,4,128,256]{3,2,1,0:T(8,128)(2,1)S(1)} %copy-done.2, bf16[2,4,128,256]{3,2,1,0:T(8,128)(2,1)S(1)} %copy-done.3, s32[4]{0:T(128)S(1)} %copy-done.4, s32[32]{0:T(128)S(1)} %copy-done.5, s32[8]{0:T(128)S(1)} %copy-done.6, bf16[2,512,512]{2,1,0:T(8,128)(2,1)S(1)} %copy-done.1, ...), custom_call_target="tpu_custom_call" | custom-call | tf_op jit(solution)/shard_map/pallas_call | solution.py:524
  71.1 0.8 %copy.9 = bf16[2,4,128,256]{3,2,1,0:T(8,128)(2,1)} copy(bf16[2,4,128,256]{3,2,1,0:T(8,128)(2,1)S(1)} %shard_map.73) | data formatting | bytes 1048576
Async XLA Ops:
  0.0 1.2 %copy-start = (bf16[2,512,512]{2,1,0:T(8,128)(2,1)S(1)}, bf16[2,512,512]{2,1,0:T(8,128)(2,1)}, u32[]{:S(2)}) copy-start(bf16[2,512,512]{2,1,0:T(8,128)(2,1)} %constant.5.clone.inverse_hbm) | copy-start | bytes 3145732
  1.2 1.2 %copy-start.1 = (bf16[2,512,512]{2,1,0:T(8,128)(2,1)S(1)}, bf16[2,512,512]{2,1,0:T(8,128)(2,1)}, u32[]{:S(2)}) copy-start(bf16[2,512,512]{2,1,0:T(8,128)(2,1)} %constant.4.clone.forward_hbm) | copy-start | bytes 3145732
  2.5 1.0 %copy-start.2 = (bf16[2,4,128,256]{3,2,1,0:T(8,128)(2,1)S(1)}, bf16[2,4,128,256]{3,2,1,0:T(8,128)(2,1)}, u32[]{:S(2)}) copy-start(bf16[2,4,128,256]{3,2,1,0:T(8,128)(2,1)} %blended_ref.1) | copy-start | bytes 1572868
  3.5 1.0 %copy-start.3 = (bf16[2,4,128,256]{3,2,1,0:T(8,128)(2,1)S(1)}, bf16[2,4,128,256]{3,2,1,0:T(8,128)(2,1)}, u32[]{:S(2)}) copy-start(bf16[2,4,128,256]{3,2,1,0:T(8,128)(2,1)} %estimate_ref.1) | copy-start | bytes 1572868
  4.5 0.7 copy-start.4
  5.2 0.7 copy-start.5
  5.8 0.7 copy-start.6
where the time goes:
time: 72.2 us; the launch traced here: 71.9 us
  Pallas kernels  64.5 us (89%)
  local copies, waits for them, and re-layouts  7.29 us (10%)
    pallas_call x1, Pallas kernels, in_one_kernel(): pl.pallas_call(functools.partial(deblend_kernel, n, nf, block, few, nr),...  64.5 us
    unnamed x15, local copies, waits for them, and re-layouts  7.29 us

commit v1 on v0

--- a/solution.py
+++ b/solution.py
@@ -148,17 +148,15 @@
 
 
 def fourier_matrices(length):
-    indices = np.arange(length)
-    angles = 2.0 * np.pi / length * (np.outer(indices, indices) % length)
-    cos, sin = np.cos(angles), np.sin(angles)
-    forward = np.block([[cos, -sin], [sin, cos]])
-
-    def split(matrix):
-        hi = matrix.astype(jnp.bfloat16)
-        lo = (matrix - hi.astype(np.float64)).astype(jnp.bfloat16)
-        return np.stack([hi, lo])
-
-    return split(forward), split(forward.T)
+    half = np.arange(length // 2)
+
+    def turns(parity):
+        angles = 2.0 * np.pi / length * (np.outer(half, 2 * half + parity) % length)
+        cos, sin = np.cos(angles), np.sin(angles)
+        return np.block([[cos, -sin], [sin, cos]])
+
+    forward = np.stack([turns(0), turns(1)]).astype(np.float32)
+    return np.stack([forward, np.swapaxes(forward, 1, 2)])
 
 
 def short_fourier(values, sign):
@@ -203,12 +201,14 @@
     nr,
     blended_ref,
     estimate_ref,
+    partner_hbm,
+    delays_hbm,
+    levels_hbm,
+    tables_hbm,
+    out_ref,
     partner_ref,
     delays_ref,
     levels_ref,
-    forward_hbm,
-    inverse_hbm,
-    out_ref,
     e_all,
     b_all,
     info,
@@ -223,6 +223,7 @@
     limit,
     near_sums,
     far_sums,
+    exact,
     forward,
     inverse,
     local_sem,
@@ -242,6 +243,8 @@
     total = n * block
     span = 2 * block
     half = n // 2
+    hr = nr // 2
+    columns = [parity * nr + c for parity in range(2) for c in range(0, hr, LANES)]
     me = lax.axis_index("shot")
     column = lax.axis_index("freq")
     mesh_id = pl.DeviceIdType.MESH
@@ -255,23 +258,31 @@
     for k in range(1, nf):
         pl.semaphore_signal(barrier, inc=1, device_id={"freq": others[k]}, device_id_type=mesh_id)
 
+    scalar_copies = [
+        pltpu.make_async_copy(partner_hbm, partner_ref, local_sem.at[3]),
+        pltpu.make_async_copy(delays_hbm, delays_ref, local_sem.at[4]),
+        pltpu.make_async_copy(levels_hbm, levels_ref, local_sem.at[5]),
+    ]
+    for copy in scalar_copies:
+        copy.start()
     local_copies = [
-        pltpu.make_async_copy(forward_hbm, forward, local_sem.at[0]),
-        pltpu.make_async_copy(inverse_hbm, inverse, local_sem.at[1]),
+        pltpu.make_async_copy(tables_hbm, exact, local_sem.at[0]),
         pltpu.make_async_copy(
             estimate_ref.at[:, :, pl.ds(me * few, few), :],
             e_all.at[:, pl.ds(me * block, block)],
-            local_sem.at[2],
+            local_sem.at[1],
         ),
         pltpu.make_async_copy(
             blended_ref.at[:, :, pl.ds(me * few, few), :],
             b_all.at[:, pl.ds(me * block, block)],
-            local_sem.at[3],
+            local_sem.at[2],
         ),
     ]
     for copy in local_copies:
         copy.start()
 
+    for copy in scalar_copies:
+        copy.wait()
     lane = lax.broadcasted_iota(jnp.int32, (8, LANES), 1)
     row = lax.broadcasted_iota(jnp.int32, (8, LANES), 0)
     tile = jnp.zeros((8, LANES), jnp.int32)
@@ -335,9 +346,15 @@
         turn_sin[s] = jnp.broadcast_to(sin_table[:, s : s + 1], (few, LANES))
         turn_pick[s] = jnp.broadcast_to(known[0:1, s : s + 1] - first, (few, LANES))
 
+    local_copies[0].wait()
+    for index, pair in enumerate((forward, inverse)):
+        top = exact[index].astype(jnp.bfloat16)
+        pair[0] = top
+        pair[1] = (exact[index] - top.astype(jnp.float32)).astype(jnp.bfloat16)
+
     for copy in record_copies:
         copy.wait()
-    for copy in local_copies:
+    for copy in local_copies[1:]:
         copy.wait()
 
     def keep(s, lanes, value):
@@ -346,61 +363,79 @@
         x_lo[s, :, lanes] = (value - top.astype(jnp.float32)).astype(jnp.bfloat16)
 
     def relax(pair, carried):
-        for c in range(0, nr, LANES):
-            lanes = slice(c, c + LANES)
-            records = [
-                [
-                    [
-                        e_all[part, (pair + side * half) * block + i, :, lanes].astype(jnp.float32)
-                        for part in range(2)
-                    ]
-                    for i in range(block)
-                ]
-                for side in range(2)
-            ]
+        for c in range(0, hr, LANES):
+            halves = (slice(c, c + LANES), slice(hr + c, hr + c + LANES))
             for side in range(2):
+                first = (pair + side * half) * block
+                other = (pair + (1 - side) * half) * block
                 for i in range(block):
-                    s = (pair + side * half) * block + i
+                    s = first + i
                     pick = turn_pick[s]
                     cos, sin = turn_cos[s], turn_sin[s]
-                    mate_real, mate_imag = records[1 - side][0]
-                    for j in range(1, block):
-                        mate_real = jnp.where(pick == j, records[1 - side][j][0], mate_real)
-                        mate_imag = jnp.where(pick == j, records[1 - side][j][1], mate_imag)
-                    real, imag = records[side][i]
-                    seen_real = b_all[0, s, :, lanes].astype(jnp.float32)
-                    seen_imag = b_all[1, s, :, lanes].astype(jnp.float32)
-                    keep(
-                        s,
-                        lanes,
-                        real + relaxation * (seen_real - real) - (mate_real * cos + mate_imag * sin),
-                    )
-                    keep(
-                        s,
-                        slice(nr + c, nr + c + LANES),
-                        imag + relaxation * (seen_imag - imag) - (mate_imag * cos - mate_real * sin),
-                    )
+                    moved = []
+                    for lanes in halves:
+                        mate_real = e_all[0, other, :, lanes].astype(jnp.float32)
+                        mate_imag = e_all[1, other, :, lanes].astype(jnp.float32)
+                        for j in range(1, block):
+                            here = pick == j
+                            real = e_all[0, other + j, :, lanes].astype(jnp.float32)
+                            imag = e_all[1, other + j, :, lanes].astype(jnp.float32)
+                            mate_real = jnp.where(here, real, mate_real)
+                            mate_imag = jnp.where(here, imag, mate_imag)
+                        real = e_all[0, s, :, lanes].astype(jnp.float32)
+                        imag = e_all[1, s, :, lanes].astype(jnp.float32)
+                        seen_real = b_all[0, s, :, lanes].astype(jnp.float32)
+                        seen_imag = b_all[1, s, :, lanes].astype(jnp.float32)
+                        shift_real = mate_real * cos + mate_imag * sin
+                        shift_imag = mate_imag * cos - mate_real * sin
+                        moved.append(
+                            (
+                                real + relaxation * (seen_real - real) - shift_real,
+                                imag + relaxation * (seen_imag - imag) - shift_imag,
+                            )
+                        )
+                    for part in range(2):
+                        at = part * hr + c
+                        keep(s, slice(at, at + LANES), moved[0][part] + moved[1][part])
+                        at = nr + at
+                        keep(s, slice(at, at + LANES), moved[0][part] - moved[1][part])
         return carried
 
     def receivers(start, table):
         rows = (total // 2) * few
-        top = x_hi[pl.ds(start, total // 2)].reshape(rows, 2 * nr)
-        rest = x_lo[pl.ds(start, total // 2)].reshape(rows, 2 * nr)
-        result = jnp.dot(top, table[0], preferred_element_type=jnp.float32)
-        result = result + jnp.dot(rest, table[0], preferred_element_type=jnp.float32)
-        result = result + jnp.dot(top, table[1], preferred_element_type=jnp.float32)
-        return result.reshape(total // 2, few, 2 * nr)
+        results = []
+        for parity in range(2):
+            lanes = slice(parity * nr, (parity + 1) * nr)
+            top = x_hi[pl.ds(start, total // 2), :, lanes].reshape(rows, nr)
+            rest = x_lo[pl.ds(start, total // 2), :, lanes].reshape(rows, nr)
+            result = jnp.dot(top, table[0, parity], preferred_element_type=jnp.float32)
+            result = result + jnp.dot(rest, table[0, parity], preferred_element_type=jnp.float32)
+            result = result + jnp.dot(top, table[1, parity], preferred_element_type=jnp.float32)
+            results.append(result.reshape(total // 2, few, nr))
+        return results
+
+    def to_lines(start):
+        for parity, result in enumerate(receivers(start, forward)):
+            lines[pl.ds(start, total // 2), :, parity * nr : (parity + 1) * nr] = result
+
+    def to_estimate(start):
+        even, odd = receivers(start, inverse)
+        for lanes, result in ((slice(0, hr), even + odd), (slice(hr, nr), even - odd)):
+            for part in range(2):
+                e_all[part, pl.ds(start, total // 2), :, lanes] = result[
+                    :, :, part * hr : (part + 1) * hr
+                ].astype(jnp.bfloat16)
 
     weights = [math.sin(math.pi * (t + 0.5) / span) ** 2 for t in range(span)]
 
     def analyse(step):
         def window(j, carried):
             summed = jnp.zeros((few, LANES), jnp.float32)
-            for c in range(0, nr, LANES):
+            for c in columns:
                 values = [
                     (
                         lines[j * block + t, :, c : c + LANES] * weights[t],
-                        lines[j * block + t, :, nr + c : nr + c + LANES] * weights[t],
+                        lines[j * block + t, :, hr + c : hr + c + LANES] * weights[t],
                     )
                     for t in range(span)
                 ]
@@ -408,7 +443,7 @@
                     power = real * real + imag * imag
                     summed = summed + power * lax.rsqrt(jnp.maximum(power, TINY))
                     coefs[j, k, :, c : c + LANES] = real
-                    coefs[j, k, :, nr + c : nr + c + LANES] = imag
+                    coefs[j, k, :, hr + c : hr + c + LANES] = imag
             near_sums[step, 0, pl.ds(j, 1), :] = jnp.sum(summed, axis=0, keepdims=True)
             return carried
 
@@ -453,17 +488,17 @@
     def synthesise(j, carried):
         level = levels_ref[j].astype(jnp.float32) * (level_scale * scale / count)
         bound = limit[pl.ds(j, 1), :] * level
-        for c in range(0, nr, LANES):
+        for c in columns:
             values = []
             for k in range(span):
                 real = coefs[j, k, :, c : c + LANES]
-                imag = coefs[j, k, :, nr + c : nr + c + LANES]
+                imag = coefs[j, k, :, hr + c : hr + c + LANES]
                 power = real * real + imag * imag
                 factor = jnp.maximum(scale - bound * lax.rsqrt(power), 0.0)
                 values.append((real * factor, imag * factor))
             for t, parts in enumerate(short_fourier(values, 1)):
                 for part in range(2):
-                    lanes = slice(part * nr + c, part * nr + c + LANES)
+                    lanes = slice(part * hr + c, part * hr + c + LANES)
                     if t < block:
                         keep(j * block + t, lanes, parts[part] + carry[t, :, lanes])
                     else:
@@ -473,24 +508,20 @@
     for step in range(PASSES):
         lax.fori_loop(0, half, relax, 0)
         for start in (0, total // 2):
-            lines[pl.ds(start, total // 2)] = receivers(start, forward)
+            to_lines(start)
         analyse(step)
         thresholds(step)
         carry[...] = jnp.zeros_like(carry)
         lax.fori_loop(0, n, synthesise, 0)
         if step < PASSES - 1:
             for start in (0, total // 2):
-                result = receivers(start, inverse).astype(jnp.bfloat16)
-                e_all[0, pl.ds(start, total // 2)] = result[:, :, :nr]
-                e_all[1, pl.ds(start, total // 2)] = result[:, :, nr:]
+                to_estimate(start)
 
     copies = []
     mine = me // half
     for side, group in ((1 - mine, range(half, n)), (mine, range(1, half))):
         start = side * (total // 2)
-        result = receivers(start, inverse).astype(jnp.bfloat16)
-        e_all[0, pl.ds(start, total // 2)] = result[:, :, :nr]
-        e_all[1, pl.ds(start, total // 2)] = result[:, :, nr:]
+        to_estimate(start)
         for k in group:
             copies.append(
                 send(
@@ -516,17 +547,19 @@
     block, freq_local, nr = estimate.shape[1:]
     few = freq_local // n
     total = n * block
-    forward, inverse = fourier_matrices(nr)
+    tables_both = fourier_matrices(nr)
     f32, bf16 = jnp.float32, jnp.bfloat16
     anywhere = pl.BlockSpec(memory_space=pl.ANY)
-    scalars = pl.BlockSpec(memory_space=pltpu.SMEM)
     dma = pltpu.SemaphoreType.DMA
     return pl.pallas_call(
         functools.partial(deblend_kernel, n, nf, block, few, nr),
         out_shape=jax.ShapeDtypeStruct(estimate.shape, estimate.dtype),
-        in_specs=[anywhere, anywhere, scalars, scalars, scalars, anywhere, anywhere],
+        in_specs=[anywhere] * 6,
         out_specs=anywhere,
         scratch_shapes=[
+            pltpu.SMEM(partner.shape, jnp.int32),
+            pltpu.SMEM(delays.shape, jnp.int32),
+            pltpu.SMEM(levels.shape, jnp.int32),
             pltpu.VMEM((2, total, few, nr), bf16),
             pltpu.VMEM((2, total, few, nr), bf16),
             pltpu.VMEM((n, 8, LANES), jnp.int32),
@@ -541,9 +574,10 @@
             pltpu.VMEM((n, LANES), f32),
             pltpu.VMEM((PASSES, n, n, LANES), f32),
             pltpu.VMEM((PASSES, nf, n, LANES), f32),
-            pltpu.VMEM(forward.shape, bf16),
-            pltpu.VMEM(inverse.shape, bf16),
-            dma((4,)),
+            pltpu.VMEM(tables_both.shape, f32),
+            pltpu.VMEM(tables_both.shape, bf16),
+            pltpu.VMEM(tables_both.shape, bf16),
+            dma((6,)),
             dma((n,)),
             dma((n,)),
             dma((n,)),
@@ -558,9 +592,9 @@
             dma((n,)),
         ],
         compiler_params=pltpu.CompilerParams(
-            collective_id=0, has_side_effects=True, vmem_limit_bytes=48 * 1024 * 1024
+            collective_id=0, has_side_effects=True, vmem_limit_bytes=60 * 1024 * 1024
         ),
-    )(blended, estimate, partner, delays, levels, jnp.asarray(forward), jnp.asarray(inverse))
+    )(blended, estimate, partner, delays, levels, jnp.asarray(tables_both))
 
 
 def solution(mesh):
@@ -569,7 +603,7 @@
     def body(blended, estimate, partner, delays, levels):
         block, freq_local, nr = estimate.shape[1:]
         whole_tiles = (
-            n == 8 and freq_local % (16 * n) == 0 and nr % LANES == 0 and n * block <= LANES
+            n == 8 and freq_local % (16 * n) == 0 and nr % (2 * LANES) == 0 and n * block <= LANES
         )
         if whole_tiles:
             return in_one_kernel(n, nf, blended, estimate, partner, delays, levels)

time: 72.2 us -> 64.9 us (0.90)
  local copies, waits for them, and re-layouts: 7.29 us -> 1.87 us
  Pallas kernels: 64.5 us -> 62.8 us
    unnamed x15 -> x1, local copies, waits for them, and re-layouts: 7.29 us -> 1.87 us
    pallas_call x1, Pallas kernels: 64.5 us -> 62.8 us  [in_one_kernel(): pl.pallas_call(functools.partial(deblend_kernel, n, nf, block, few, nr),...]
where the time goes in v1:
time: 64.9 us; the launch traced here: 64.7 us
  Pallas kernels  62.8 us (97%)
  local copies, waits for them, and re-layouts  1.87 us (3%)
    pallas_call x1, Pallas kernels, in_one_kernel(): pl.pallas_call(functools.partial(deblend_kernel, n, nf, block, few, nr),...  62.8 us
    unnamed x1, local copies, waits for them, and re-layouts  1.87 us

profile of v1, /device:TPU:0, one launch (start us, length us, event | category | flops | bytes accessed | tf_op | source)
XLA Modules:
  0.0 64.7 jit_solution(14285694112314542681)
XLA Ops:
  0.0 62.8 %shard_map.64 = bf16[2,4,128,256]{3,2,1,0:T(8,128)(2,1)} custom-call(bf16[2,4,128,256]{3,2,1,0:T(8,128)(2,1)} %blended_ref.1, bf16[2,4,128,256]{3,2,1,0:T(8,128)(2,1)} %estimate_ref.1, s32[4]{0:T(128)} %partner_hbm.1, s32[32]{0:T(128)} %delays_hbm.1, s32[8]{0:T(128)} %levels_hbm.1, f32[2,2,256,256]{3,2,1,0:T(8,128)} %constant.2.clone.tables_hbm), custom_call_target="tpu_custom_call" | custom-call | tf_op jit(solution)/shard_map/pallas_call | solution.py:554
  62.8 1.9 %copy.8 = bf16[2,4,128,256]{3,2,1,0:T(8,128)(2,1)} copy(bf16[2,4,128,256]{3,2,1,0:T(8,128)(2,1)} %shard_map.64) | data formatting | bytes 1048576

commit v2 on v1

--- a/solution.py
+++ b/solution.py
@@ -221,8 +221,7 @@
     coefs,
     carry,
     limit,
-    near_sums,
-    far_sums,
+    sums,
     exact,
     forward,
     inverse,
@@ -233,10 +232,8 @@
     e_recv,
     b_send,
     b_recv,
-    near_send,
-    near_recv,
-    far_send,
-    far_recv,
+    sums_send,
+    sums_recv,
     out_send,
     out_recv,
 ):
@@ -249,14 +246,14 @@
     column = lax.axis_index("freq")
     mesh_id = pl.DeviceIdType.MESH
     peers = [flipped(me, k, n) for k in range(n)]
-    order = list(range(half, n)) + list(range(1, half))
+    order = [half] + [k for near in range(1, half) for k in (near + half, near)]
     others = [lax.rem(column + k, nf) for k in range(nf)]
+    everyone = [(k, f) for k in order + [0] for f in range(nf) if (k, f) != (0, 0)]
 
     barrier = pltpu.get_barrier_semaphore()
-    for k in order:
-        pl.semaphore_signal(barrier, inc=1, device_id={"shot": peers[k]}, device_id_type=mesh_id)
-    for k in range(1, nf):
-        pl.semaphore_signal(barrier, inc=1, device_id={"freq": others[k]}, device_id_type=mesh_id)
+    for k, f in everyone:
+        where = {"shot": peers[k], "freq": others[f]}
+        pl.semaphore_signal(barrier, inc=1, device_id=where, device_id_type=mesh_id)
 
     scalar_copies = [
         pltpu.make_async_copy(partner_hbm, partner_ref, local_sem.at[3]),
@@ -295,7 +292,7 @@
         tile = jnp.where(here & (row == 1), offset, tile)
     info[0] = tile
 
-    pl.semaphore_wait(barrier, n + nf - 2)
+    pl.semaphore_wait(barrier, n * nf - 1)
 
     def send(source, target, send_sem, recv_sem, where):
         copy = pltpu.make_async_remote_copy(
@@ -313,13 +310,14 @@
         send(info.at[0], info.at[k], info_send.at[k], info_recv.at[k], {"shot": peers[k]})
         for k in order
     ]
-    record_copies = []
+    record_copies = {k: [] for k in range(n)}
+    record_copies[0] = local_copies[1:]
     for k in order:
         for held, whole, sent, received in (
             (estimate_ref, e_all, e_send, e_recv),
             (blended_ref, b_all, b_send, b_recv),
         ):
-            record_copies.append(
+            record_copies[k].append(
                 send(
                     held.at[:, :, pl.ds(peers[k] * few, few), :],
                     whole.at[:, pl.ds(me * block, block)],
@@ -351,11 +349,6 @@
         top = exact[index].astype(jnp.bfloat16)
         pair[0] = top
         pair[1] = (exact[index] - top.astype(jnp.float32)).astype(jnp.bfloat16)
-
-    for copy in record_copies:
-        copy.wait()
-    for copy in local_copies[1:]:
-        copy.wait()
 
     def keep(s, lanes, value):
         top = value.astype(jnp.bfloat16)
@@ -394,35 +387,40 @@
                                 imag + relaxation * (seen_imag - imag) - shift_imag,
                             )
                         )
+                    place = (2 * pair + side) * block + i
                     for part in range(2):
                         at = part * hr + c
-                        keep(s, slice(at, at + LANES), moved[0][part] + moved[1][part])
+                        keep(place, slice(at, at + LANES), moved[0][part] + moved[1][part])
                         at = nr + at
-                        keep(s, slice(at, at + LANES), moved[0][part] - moved[1][part])
+                        keep(place, slice(at, at + LANES), moved[0][part] - moved[1][part])
         return carried
 
-    def receivers(start, table):
-        rows = (total // 2) * few
+    def receivers(start, shots, table):
         results = []
         for parity in range(2):
             lanes = slice(parity * nr, (parity + 1) * nr)
-            top = x_hi[pl.ds(start, total // 2), :, lanes].reshape(rows, nr)
-            rest = x_lo[pl.ds(start, total // 2), :, lanes].reshape(rows, nr)
+            top = x_hi[pl.ds(start, shots), :, lanes].reshape(shots * few, nr)
+            rest = x_lo[pl.ds(start, shots), :, lanes].reshape(shots * few, nr)
             result = jnp.dot(top, table[0, parity], preferred_element_type=jnp.float32)
             result = result + jnp.dot(rest, table[0, parity], preferred_element_type=jnp.float32)
             result = result + jnp.dot(top, table[1, parity], preferred_element_type=jnp.float32)
-            results.append(result.reshape(total // 2, few, nr))
+            results.append(result.reshape(shots, few, nr))
         return results
 
-    def to_lines(start):
-        for parity, result in enumerate(receivers(start, forward)):
-            lines[pl.ds(start, total // 2), :, parity * nr : (parity + 1) * nr] = result
-
-    def to_estimate(start):
-        even, odd = receivers(start, inverse)
+    def to_lines(pair, pairs):
+        for parity, result in enumerate(receivers(pair * span, pairs * span, forward)):
+            lanes = slice(parity * nr, (parity + 1) * nr)
+            for p in range(pairs):
+                for side in range(2):
+                    at = (2 * p + side) * block
+                    target = pl.ds((pair + p + side * half) * block, block)
+                    lines[target, :, lanes] = result[at : at + block]
+
+    def to_estimate(start, shots):
+        even, odd = receivers(start, shots, inverse)
         for lanes, result in ((slice(0, hr), even + odd), (slice(hr, nr), even - odd)):
             for part in range(2):
-                e_all[part, pl.ds(start, total // 2), :, lanes] = result[
+                e_all[part, pl.ds(start, shots), :, lanes] = result[
                     :, :, part * hr : (part + 1) * hr
                 ].astype(jnp.bfloat16)
 
@@ -444,43 +442,33 @@
                     summed = summed + power * lax.rsqrt(jnp.maximum(power, TINY))
                     coefs[j, k, :, c : c + LANES] = real
                     coefs[j, k, :, hr + c : hr + c + LANES] = imag
-            near_sums[step, 0, pl.ds(j, 1), :] = jnp.sum(summed, axis=0, keepdims=True)
+            limit[pl.ds(j, 1), :] = jnp.sum(summed, axis=0, keepdims=True)
             return carried
 
         lax.fori_loop(0, n, window, 0)
 
+    diagonal = lax.broadcasted_iota(jnp.int32, (n, LANES), 0) == lax.broadcasted_iota(
+        jnp.int32, (n, LANES), 1
+    )
+
     def thresholds(step):
+        column_sums = jnp.sum(limit[...], axis=1, keepdims=True)
+        sums[step, 0] = jnp.sum(jnp.where(diagonal, column_sums, 0.0), axis=0, keepdims=True)
         copies = [
             send(
-                near_sums.at[step, 0],
-                near_sums.at[step, k],
-                near_send.at[step, k],
-                near_recv.at[step, k],
-                {"shot": peers[k]},
+                sums.at[step, 0],
+                sums.at[step, k * nf + f],
+                sums_send.at[step, k * nf + f],
+                sums_recv.at[step, k * nf + f],
+                {"shot": peers[k], "freq": others[f]},
             )
-            for k in order
+            for k, f in everyone
         ]
         for copy in copies:
             copy.wait()
-        part = near_sums[step, 0]
-        for k in range(1, n):
-            part = part + near_sums[step, k]
-        far_sums[step, 0] = part
-        copies = [
-            send(
-                far_sums.at[step, 0],
-                far_sums.at[step, k],
-                far_send.at[step, k],
-                far_recv.at[step, k],
-                {"freq": others[k]},
-            )
-            for k in range(1, nf)
-        ]
-        for copy in copies:
-            copy.wait()
-        for k in range(1, nf):
-            part = part + far_sums[step, k]
-        limit[...] = jnp.broadcast_to(jnp.sum(part, axis=1, keepdims=True), (n, LANES))
+        whole = jnp.sum(sums[step], axis=0)
+        column_sums = jnp.sum(jnp.where(diagonal, whole, 0.0), axis=1, keepdims=True)
+        limit[...] = jnp.broadcast_to(column_sums, (n, LANES))
 
     scale = 1.0 / (span * nr)
     count = span * few * n * nf * nr
@@ -506,32 +494,39 @@
         return carried
 
     for step in range(PASSES):
-        lax.fori_loop(0, half, relax, 0)
-        for start in (0, total // 2):
-            to_lines(start)
+        if step == 0:
+            for near in range(half):
+                for copy in record_copies[near] + record_copies[near + half]:
+                    copy.wait()
+                pair = peers[near] % half
+                relax(pair, 0)
+                to_lines(pair, 1)
+        else:
+            lax.fori_loop(0, half, relax, 0)
+            for pair in range(0, half, half // 2):
+                to_lines(pair, half // 2)
         analyse(step)
         thresholds(step)
         carry[...] = jnp.zeros_like(carry)
         lax.fori_loop(0, n, synthesise, 0)
         if step < PASSES - 1:
             for start in (0, total // 2):
-                to_estimate(start)
+                to_estimate(start, total // 2)
 
     copies = []
-    mine = me // half
-    for side, group in ((1 - mine, range(half, n)), (mine, range(1, half))):
-        start = side * (total // 2)
-        to_estimate(start)
+    for group in [(k, k + 1) for k in range(half, n, 2)] + [(2, 3), (0, 1)]:
+        to_estimate(peers[group[0]] // 2 * 2 * block, 2 * block)
         for k in group:
-            copies.append(
-                send(
-                    e_all.at[:, pl.ds(peers[k] * block, block)],
-                    out_ref.at[:, :, pl.ds(me * few, few), :],
-                    out_send.at[k],
-                    out_recv.at[k],
-                    {"shot": peers[k]},
+            if k:
+                copies.append(
+                    send(
+                        e_all.at[:, pl.ds(peers[k] * block, block)],
+                        out_ref.at[:, :, pl.ds(me * few, few), :],
+                        out_send.at[k],
+                        out_recv.at[k],
+                        {"shot": peers[k]},
+                    )
                 )
-            )
     last = pltpu.make_async_copy(
         e_all.at[:, pl.ds(me * block, block)],
         out_ref.at[:, :, pl.ds(me * few, few), :],
@@ -572,8 +567,7 @@
             pltpu.VMEM((n, 2 * block, few, 2 * nr), f32),
             pltpu.VMEM((block, few, 2 * nr), f32),
             pltpu.VMEM((n, LANES), f32),
-            pltpu.VMEM((PASSES, n, n, LANES), f32),
-            pltpu.VMEM((PASSES, nf, n, LANES), f32),
+            pltpu.VMEM((PASSES, n * nf, 1, LANES), f32),
             pltpu.VMEM(tables_both.shape, f32),
             pltpu.VMEM(tables_both.shape, bf16),
             pltpu.VMEM(tables_both.shape, bf16),
@@ -584,10 +578,8 @@
             dma((n,)),
             dma((n,)),
             dma((n,)),
-            dma((PASSES, n)),
-            dma((PASSES, n)),
-            dma((PASSES, nf)),
-            dma((PASSES, nf)),
+            dma((PASSES, n * nf)),
+            dma((PASSES, n * nf)),
             dma((n,)),
             dma((n,)),
         ],

time: 64.9 us -> 62.1 us (0.957)
  Pallas kernels: 62.8 us -> 60 us
    pallas_call x1, Pallas kernels: 62.8 us -> 60 us  [in_one_kernel(): pl.pallas_call(functools.partial(deblend_kernel, n, nf, block, few, nr),...]
where the time goes in v2:
time: 62.1 us; the launch traced here: 61.9 us
  Pallas kernels  60 us (97%)
  local copies, waits for them, and re-layouts  1.87 us (3%)
    pallas_call x1, Pallas kernels, in_one_kernel(): pl.pallas_call(functools.partial(deblend_kernel, n, nf, block, few, nr),...  60 us
    unnamed x1, local copies, waits for them, and re-layouts  1.87 us

profile of v2, /device:TPU:0, one launch (start us, length us, event | category | flops | bytes accessed | tf_op | source)
XLA Modules:
  0.0 61.9 jit_solution(17402396026002878938)
XLA Ops:
  0.0 60.0 %shard_map.64 = bf16[2,4,128,256]{3,2,1,0:T(8,128)(2,1)} custom-call(bf16[2,4,128,256]{3,2,1,0:T(8,128)(2,1)} %blended_ref.1, bf16[2,4,128,256]{3,2,1,0:T(8,128)(2,1)} %estimate_ref.1, s32[4]{0:T(128)} %partner_hbm.1, s32[32]{0:T(128)} %delays_hbm.1, s32[8]{0:T(128)} %levels_hbm.1, f32[2,2,256,256]{3,2,1,0:T(8,128)} %constant.2.clone.tables_hbm), custom_call_target="tpu_custom_call" | custom-call | tf_op jit(solution)/shard_map/pallas_call | solution.py:549
  60.0 1.9 %copy.8 = bf16[2,4,128,256]{3,2,1,0:T(8,128)(2,1)} copy(bf16[2,4,128,256]{3,2,1,0:T(8,128)(2,1)} %shard_map.64) | data formatting | bytes 1048576

commit v3 on v2

--- a/solution.py
+++ b/solution.py
@@ -215,8 +215,7 @@
     turn_cos,
     turn_sin,
     turn_pick,
-    x_hi,
-    x_lo,
+    x,
     lines,
     coefs,
     carry,
@@ -241,7 +240,7 @@
     span = 2 * block
     half = n // 2
     hr = nr // 2
-    columns = [parity * nr + c for parity in range(2) for c in range(0, hr, LANES)]
+    columns = [(parity, c) for parity in range(2) for c in range(0, hr, LANES)]
     me = lax.axis_index("shot")
     column = lax.axis_index("freq")
     mesh_id = pl.DeviceIdType.MESH
@@ -345,15 +344,18 @@
         turn_pick[s] = jnp.broadcast_to(known[0:1, s : s + 1] - first, (few, LANES))
 
     local_copies[0].wait()
-    for index, pair in enumerate((forward, inverse)):
+    for index, stack in enumerate((forward, inverse)):
         top = exact[index].astype(jnp.bfloat16)
-        pair[0] = top
-        pair[1] = (exact[index] - top.astype(jnp.float32)).astype(jnp.bfloat16)
-
-    def keep(s, lanes, value):
+        stack[:, :nr] = top
+        stack[:, nr : 2 * nr] = top
+        stack[:, 2 * nr :] = (exact[index] - top.astype(jnp.float32)).astype(jnp.bfloat16)
+
+    def keep(s, parity, at, value):
+        start = 2 * nr * parity + at
         top = value.astype(jnp.bfloat16)
-        x_hi[s, :, lanes] = top
-        x_lo[s, :, lanes] = (value - top.astype(jnp.float32)).astype(jnp.bfloat16)
+        x[s, :, start : start + LANES] = top
+        rest = value - top.astype(jnp.float32)
+        x[s, :, start + nr : start + nr + LANES] = rest.astype(jnp.bfloat16)
 
     def relax(pair, carried):
         for c in range(0, hr, LANES):
@@ -390,20 +392,18 @@
                     place = (2 * pair + side) * block + i
                     for part in range(2):
                         at = part * hr + c
-                        keep(place, slice(at, at + LANES), moved[0][part] + moved[1][part])
-                        at = nr + at
-                        keep(place, slice(at, at + LANES), moved[0][part] - moved[1][part])
+                        keep(place, 0, at, moved[0][part] + moved[1][part])
+                        keep(place, 1, at, moved[0][part] - moved[1][part])
         return carried
 
     def receivers(start, shots, table):
         results = []
         for parity in range(2):
-            lanes = slice(parity * nr, (parity + 1) * nr)
-            top = x_hi[pl.ds(start, shots), :, lanes].reshape(shots * few, nr)
-            rest = x_lo[pl.ds(start, shots), :, lanes].reshape(shots * few, nr)
-            result = jnp.dot(top, table[0, parity], preferred_element_type=jnp.float32)
-            result = result + jnp.dot(rest, table[0, parity], preferred_element_type=jnp.float32)
-            result = result + jnp.dot(top, table[1, parity], preferred_element_type=jnp.float32)
+            start_lane = 2 * nr * parity
+            both = x[pl.ds(start, shots), :, start_lane : start_lane + 2 * nr]
+            both = both.reshape(shots * few, 2 * nr)
+            rows = jnp.concatenate([both, both[:, :nr]], axis=1)
+            result = jnp.dot(rows, table[parity], preferred_element_type=jnp.float32)
             results.append(result.reshape(shots, few, nr))
         return results
 
@@ -429,7 +429,8 @@
     def analyse(step):
         def window(j, carried):
             summed = jnp.zeros((few, LANES), jnp.float32)
-            for c in columns:
+            for parity, c in columns:
+                c += parity * nr
                 values = [
                     (
                         lines[j * block + t, :, c : c + LANES] * weights[t],
@@ -447,6 +448,7 @@
 
         lax.fori_loop(0, n, window, 0)
 
+    departures = []
     diagonal = lax.broadcasted_iota(jnp.int32, (n, LANES), 0) == lax.broadcasted_iota(
         jnp.int32, (n, LANES), 1
     )
@@ -454,18 +456,25 @@
     def thresholds(step):
         column_sums = jnp.sum(limit[...], axis=1, keepdims=True)
         sums[step, 0] = jnp.sum(jnp.where(diagonal, column_sums, 0.0), axis=0, keepdims=True)
-        copies = [
+        for k, f in everyone:
             send(
                 sums.at[step, 0],
                 sums.at[step, k * nf + f],
-                sums_send.at[step, k * nf + f],
-                sums_recv.at[step, k * nf + f],
+                sums_send.at[step],
+                sums_recv.at[step],
                 {"shot": peers[k], "freq": others[f]},
             )
-            for k, f in everyone
-        ]
-        for copy in copies:
-            copy.wait()
+        rows = sums.at[step, pl.ds(1, n * nf - 1)]
+        arrived = pltpu.make_async_remote_copy(
+            src_ref=rows,
+            dst_ref=rows,
+            send_sem=sums_send.at[step],
+            recv_sem=sums_recv.at[step],
+            device_id={"shot": peers[1]},
+            device_id_type=mesh_id,
+        )
+        arrived.wait_recv()
+        departures.append(arrived)
         whole = jnp.sum(sums[step], axis=0)
         column_sums = jnp.sum(jnp.where(diagonal, whole, 0.0), axis=1, keepdims=True)
         limit[...] = jnp.broadcast_to(column_sums, (n, LANES))
@@ -476,7 +485,8 @@
     def synthesise(j, carried):
         level = levels_ref[j].astype(jnp.float32) * (level_scale * scale / count)
         bound = limit[pl.ds(j, 1), :] * level
-        for c in columns:
+        for parity, c in columns:
+            c += parity * nr
             values = []
             for k in range(span):
                 real = coefs[j, k, :, c : c + LANES]
@@ -488,7 +498,8 @@
                 for part in range(2):
                     lanes = slice(part * hr + c, part * hr + c + LANES)
                     if t < block:
-                        keep(j * block + t, lanes, parts[part] + carry[t, :, lanes])
+                        value = parts[part] + carry[t, :, lanes]
+                        keep(j * block + t, parity, part * hr + c - parity * nr, value)
                     else:
                         carry[t - block, :, lanes] = parts[part]
         return carried
@@ -535,6 +546,8 @@
     last.start()
     for copy in copies:
         copy.wait()
+    for copy in departures:
+        copy.wait_send()
     last.wait()
 
 
@@ -544,13 +557,13 @@
     total = n * block
     tables_both = fourier_matrices(nr)
     f32, bf16 = jnp.float32, jnp.bfloat16
-    anywhere = pl.BlockSpec(memory_space=pl.ANY)
+    in_hbm = pl.BlockSpec(memory_space=pltpu.HBM)
     dma = pltpu.SemaphoreType.DMA
     return pl.pallas_call(
         functools.partial(deblend_kernel, n, nf, block, few, nr),
         out_shape=jax.ShapeDtypeStruct(estimate.shape, estimate.dtype),
-        in_specs=[anywhere] * 6,
-        out_specs=anywhere,
+        in_specs=[in_hbm] * 6,
+        out_specs=pl.BlockSpec(memory_space=pl.ANY),
         scratch_shapes=[
             pltpu.SMEM(partner.shape, jnp.int32),
             pltpu.SMEM(delays.shape, jnp.int32),
@@ -561,16 +574,15 @@
             pltpu.VMEM((total, few, LANES), f32),
             pltpu.VMEM((total, few, LANES), f32),
             pltpu.VMEM((total, few, LANES), jnp.int32),
-            pltpu.VMEM((total, few, 2 * nr), bf16),
-            pltpu.VMEM((total, few, 2 * nr), bf16),
+            pltpu.VMEM((total, few, 4 * nr), bf16),
             pltpu.VMEM((total + block, few, 2 * nr), f32),
             pltpu.VMEM((n, 2 * block, few, 2 * nr), f32),
             pltpu.VMEM((block, few, 2 * nr), f32),
             pltpu.VMEM((n, LANES), f32),
             pltpu.VMEM((PASSES, n * nf, 1, LANES), f32),
             pltpu.VMEM(tables_both.shape, f32),
-            pltpu.VMEM(tables_both.shape, bf16),
-            pltpu.VMEM(tables_both.shape, bf16),
+            pltpu.VMEM((2, 3 * nr, nr), bf16),
+            pltpu.VMEM((2, 3 * nr, nr), bf16),
             dma((6,)),
             dma((n,)),
             dma((n,)),
@@ -578,13 +590,13 @@
             dma((n,)),
             dma((n,)),
             dma((n,)),
-            dma((PASSES, n * nf)),
-            dma((PASSES, n * nf)),
+            dma((PASSES,)),
+            dma((PASSES,)),
             dma((n,)),
             dma((n,)),
         ],
         compiler_params=pltpu.CompilerParams(
-            collective_id=0, has_side_effects=True, vmem_limit_bytes=60 * 1024 * 1024
+            collective_id=0, has_side_effects=True, vmem_limit_bytes=40 * 1024 * 1024
         ),
     )(blended, estimate, partner, delays, levels, jnp.asarray(tables_both))
 

time: 62.1 us -> 65 us (1.047)
  local copies, waits for them, and re-layouts: 1.87 us -> 6.07 us
  Pallas kernels: 60 us -> 58.6 us
    unnamed x1 -> x13, local copies, waits for them, and re-layouts: 1.87 us -> 6.07 us
    pallas_call x1, Pallas kernels: 60 us -> 58.6 us  [in_one_kernel(): pl.pallas_call(functools.partial(deblend_kernel, n, nf, block, few, nr),...]
where the time goes in v3:
time: 65 us; the launch traced here: 64.7 us
  Pallas kernels  58.6 us (90%)
  local copies, waits for them, and re-layouts  6.07 us (9%)
    pallas_call x1, Pallas kernels, in_one_kernel(): pl.pallas_call(functools.partial(deblend_kernel, n, nf, block, few, nr),...  58.6 us
    unnamed x13, local copies, waits for them, and re-layouts  6.07 us

profile of v3, /device:TPU:0, one launch (start us, length us, event | category | flops | bytes accessed | tf_op | source)
XLA Modules:
  0.0 64.7 jit_solution(16581573993527998635)
XLA Ops:
  0.0 0.0 copy-start
  0.0 1.2 %copy-done = f32[2,2,256,256]{3,2,1,0:T(8,128)S(1)} copy-done((f32[2,2,256,256]{3,2,1,0:T(8,128)S(1)}, f32[2,2,256,256]{3,2,1,0:T(8,128)}, u32[]{:S(2)}) %copy-start) | copy-done | bytes 1048600
  1.2 0.0 copy-start.1
  1.2 1.0 %copy-done.1 = bf16[2,4,128,256]{3,2,1,0:T(8,128)(2,1)S(1)} copy-done((bf16[2,4,128,256]{3,2,1,0:T(8,128)(2,1)S(1)}, bf16[2,4,128,256]{3,2,1,0:T(8,128)(2,1)}, u32[]{:S(2)}) %copy-start.1) | copy-done | bytes 524312
  2.3 0.0 copy-start.2
  2.3 1.0 %copy-done.2 = bf16[2,4,128,256]{3,2,1,0:T(8,128)(2,1)S(1)} copy-done((bf16[2,4,128,256]{3,2,1,0:T(8,128)(2,1)S(1)}, bf16[2,4,128,256]{3,2,1,0:T(8,128)(2,1)}, u32[]{:S(2)}) %copy-start.2) | copy-done | bytes 524312
  3.3 0.0 copy-start.3
  3.3 0.7 %copy-done.3 = s32[4]{0:T(128)S(1)} copy-done((s32[4]{0:T(128)S(1)}, s32[4]{0:T(128)}, u32[]{:S(2)}) %copy-start.3) | copy-done | bytes 40
  4.0 0.0 copy-start.4
  4.0 0.7 %copy-done.4 = s32[32]{0:T(128)S(1)} copy-done((s32[32]{0:T(128)S(1)}, s32[32]{0:T(128)}, u32[]{:S(2)}) %copy-start.4) | copy-done | bytes 152
  4.6 0.0 copy-start.5
  4.6 0.7 %copy-done.5 = s32[8]{0:T(128)S(1)} copy-done((s32[8]{0:T(128)S(1)}, s32[8]{0:T(128)}, u32[]{:S(2)}) %copy-start.5) | copy-done | bytes 56
  5.3 58.6 %shard_map.64 = bf16[2,4,128,256]{3,2,1,0:T(8,128)(2,1)S(1)} custom-call(bf16[2,4,128,256]{3,2,1,0:T(8,128)(2,1)S(1)} %copy-done.1, bf16[2,4,128,256]{3,2,1,0:T(8,128)(2,1)S(1)} %copy-done.2, s32[4]{0:T(128)S(1)} %copy-done.3, s32[32]{0:T(128)S(1)} %copy-done.4, s32[8]{0:T(128)S(1)} %copy-done.5, f32[2,2,256,256]{3,2,1,0:T(8,128)S(1)} %copy-done), custom_call_target="tpu_custom_call" | custom-call | tf_op jit(solution)/shard_map/pallas_call | solution.py:562
  63.9 0.8 %copy.8 = bf16[2,4,128,256]{3,2,1,0:T(8,128)(2,1)} copy(bf16[2,4,128,256]{3,2,1,0:T(8,128)(2,1)S(1)} %shard_map.64) | data formatting | bytes 1048576
Async XLA Ops:
  0.0 1.2 %copy-start = (f32[2,2,256,256]{3,2,1,0:T(8,128)S(1)}, f32[2,2,256,256]{3,2,1,0:T(8,128)}, u32[]{:S(2)}) copy-start(f32[2,2,256,256]{3,2,1,0:T(8,128)} %constant.2.clone.tables_hbm) | copy-start | bytes 3145732
  1.2 1.0 %copy-start.1 = (bf16[2,4,128,256]{3,2,1,0:T(8,128)(2,1)S(1)}, bf16[2,4,128,256]{3,2,1,0:T(8,128)(2,1)}, u32[]{:S(2)}) copy-start(bf16[2,4,128,256]{3,2,1,0:T(8,128)(2,1)} %blended_ref.1) | copy-start | bytes 1572868
  2.3 1.0 %copy-start.2 = (bf16[2,4,128,256]{3,2,1,0:T(8,128)(2,1)S(1)}, bf16[2,4,128,256]{3,2,1,0:T(8,128)(2,1)}, u32[]{:S(2)}) copy-start(bf16[2,4,128,256]{3,2,1,0:T(8,128)(2,1)} %estimate_ref.1) | copy-start | bytes 1572868
  3.3 0.7 %copy-start.3 = (s32[4]{0:T(128)S(1)}, s32[4]{0:T(128)}, u32[]{:S(2)}) copy-start(s32[4]{0:T(128)} %partner_hbm.1) | copy-start | bytes 52
  4.0 0.7 %copy-start.4 = (s32[32]{0:T(128)S(1)}, s32[32]{0:T(128)}, u32[]{:S(2)}) copy-start(s32[32]{0:T(128)} %delays_hbm.1) | copy-start | bytes 388
  4.6 0.7 %copy-start.5 = (s32[8]{0:T(128)S(1)}, s32[8]{0:T(128)}, u32[]{:S(2)}) copy-start(s32[8]{0:T(128)} %levels_hbm.1) | copy-start | bytes 100

commit v4 on v3

--- a/solution.py
+++ b/solution.py
@@ -150,13 +150,14 @@
 def fourier_matrices(length):
     half = np.arange(length // 2)
 
-    def turns(parity):
-        angles = 2.0 * np.pi / length * (np.outer(half, 2 * half + parity) % length)
+    def turns(receivers, parity):
+        angles = 2.0 * np.pi / length * (np.outer(receivers, 2 * half + parity) % length)
         cos, sin = np.cos(angles), np.sin(angles)
         return np.block([[cos, -sin], [sin, cos]])
 
-    forward = np.stack([turns(0), turns(1)]).astype(np.float32)
-    return np.stack([forward, np.swapaxes(forward, 1, 2)])
+    forward = np.concatenate([turns(np.arange(length), parity) for parity in range(2)], axis=1)
+    inverse = np.stack([turns(half, parity).T for parity in range(2)])
+    return forward.astype(np.float32), inverse.astype(np.float32)
 
 
 def short_fourier(values, sign):
@@ -204,7 +205,8 @@
     partner_hbm,
     delays_hbm,
     levels_hbm,
-    tables_hbm,
+    forward_hbm,
+    inverse_hbm,
     out_ref,
     partner_ref,
     delays_ref,
@@ -214,14 +216,18 @@
     info,
     turn_cos,
     turn_sin,
-    turn_pick,
+    known_ref,
+    mates,
     x,
+    estimated,
+    observed,
     lines,
     coefs,
     carry,
     limit,
     sums,
-    exact,
+    exact_forward,
+    exact_inverse,
     forward,
     inverse,
     local_sem,
@@ -262,7 +268,8 @@
     for copy in scalar_copies:
         copy.start()
     local_copies = [
-        pltpu.make_async_copy(tables_hbm, exact, local_sem.at[0]),
+        pltpu.make_async_copy(forward_hbm, exact_forward, local_sem.at[0]),
+        pltpu.make_async_copy(inverse_hbm, exact_inverse, local_sem.at[6]),
         pltpu.make_async_copy(
             estimate_ref.at[:, :, pl.ds(me * few, few), :],
             e_all.at[:, pl.ds(me * block, block)],
@@ -310,7 +317,7 @@
         for k in order
     ]
     record_copies = {k: [] for k in range(n)}
-    record_copies[0] = local_copies[1:]
+    record_copies[0] = local_copies[2:]
     for k in order:
         for held, whole, sent, received in (
             (estimate_ref, e_all, e_send, e_recv),
@@ -337,18 +344,23 @@
     angles = 2.0 * math.pi / NT * phase.astype(jnp.float32)
     cos_table = relaxation * jnp.cos(angles)
     sin_table = relaxation * jnp.sin(angles)
+    known_ref[...] = known
+    to_scalars = pltpu.make_async_copy(known_ref, mates, local_sem.at[7])
+    to_scalars.start()
     for s in range(total):
-        first = (s // block + half) % n * block
         turn_cos[s] = jnp.broadcast_to(cos_table[:, s : s + 1], (few, LANES))
         turn_sin[s] = jnp.broadcast_to(sin_table[:, s : s + 1], (few, LANES))
-        turn_pick[s] = jnp.broadcast_to(known[0:1, s : s + 1] - first, (few, LANES))
-
-    local_copies[0].wait()
-    for index, stack in enumerate((forward, inverse)):
-        top = exact[index].astype(jnp.bfloat16)
-        stack[:, :nr] = top
-        stack[:, nr : 2 * nr] = top
-        stack[:, 2 * nr :] = (exact[index] - top.astype(jnp.float32)).astype(jnp.bfloat16)
+
+    for copy in local_copies[:2]:
+        copy.wait()
+    top = exact_forward[...].astype(jnp.bfloat16)
+    forward[: 2 * nr] = top
+    forward[2 * nr :] = (exact_forward[...] - top.astype(jnp.float32)).astype(jnp.bfloat16)
+    top = exact_inverse[...].astype(jnp.bfloat16)
+    inverse[:, :nr] = top
+    inverse[:, nr : 2 * nr] = top
+    inverse[:, 2 * nr :] = (exact_inverse[...] - top.astype(jnp.float32)).astype(jnp.bfloat16)
+    to_scalars.wait()
 
     def keep(s, parity, at, value):
         start = 2 * nr * parity + at
@@ -358,66 +370,45 @@
         x[s, :, start + nr : start + nr + LANES] = rest.astype(jnp.bfloat16)
 
     def relax(pair, carried):
-        for c in range(0, hr, LANES):
-            halves = (slice(c, c + LANES), slice(hr + c, hr + c + LANES))
-            for side in range(2):
-                first = (pair + side * half) * block
-                other = (pair + (1 - side) * half) * block
-                for i in range(block):
-                    s = first + i
-                    pick = turn_pick[s]
-                    cos, sin = turn_cos[s], turn_sin[s]
-                    moved = []
-                    for lanes in halves:
-                        mate_real = e_all[0, other, :, lanes].astype(jnp.float32)
-                        mate_imag = e_all[1, other, :, lanes].astype(jnp.float32)
-                        for j in range(1, block):
-                            here = pick == j
-                            real = e_all[0, other + j, :, lanes].astype(jnp.float32)
-                            imag = e_all[1, other + j, :, lanes].astype(jnp.float32)
-                            mate_real = jnp.where(here, real, mate_real)
-                            mate_imag = jnp.where(here, imag, mate_imag)
-                        real = e_all[0, s, :, lanes].astype(jnp.float32)
-                        imag = e_all[1, s, :, lanes].astype(jnp.float32)
-                        seen_real = b_all[0, s, :, lanes].astype(jnp.float32)
-                        seen_imag = b_all[1, s, :, lanes].astype(jnp.float32)
-                        shift_real = mate_real * cos + mate_imag * sin
-                        shift_imag = mate_imag * cos - mate_real * sin
-                        moved.append(
-                            (
-                                real + relaxation * (seen_real - real) - shift_real,
-                                imag + relaxation * (seen_imag - imag) - shift_imag,
-                            )
-                        )
-                    place = (2 * pair + side) * block + i
-                    for part in range(2):
-                        at = part * hr + c
-                        keep(place, 0, at, moved[0][part] + moved[1][part])
-                        keep(place, 1, at, moved[0][part] - moved[1][part])
+        for side in range(2):
+            for i in range(block):
+                s = (pair + side * half) * block + i
+                mate = mates[0, s]
+                cos, sin = turn_cos[s], turn_sin[s]
+                for parity, c in columns:
+                    at = parity * nr + c
+                    reals, imags = slice(at, at + LANES), slice(at + hr, at + hr + LANES)
+                    mate_real = estimated[mate, :, reals]
+                    mate_imag = estimated[mate, :, imags]
+                    seen_real = estimated[s, :, reals] + observed[s, :, reals]
+                    seen_imag = estimated[s, :, imags] + observed[s, :, imags]
+                    lines[s, :, reals] = relaxation * seen_real - (mate_real * cos + mate_imag * sin)
+                    lines[s, :, imags] = relaxation * seen_imag - (mate_imag * cos - mate_real * sin)
         return carried
 
-    def receivers(start, shots, table):
+    def to_lines(owner):
+        records = pl.ds(owner * block, block)
+        rows = []
+        for whole in (e_all, b_all):
+            real = whole[0, records].reshape(block * few, nr)
+            imag = whole[1, records].reshape(block * few, nr)
+            rows.append(jnp.concatenate([real, imag, real, imag], axis=1))
+        result = jnp.dot(
+            jnp.concatenate(rows, axis=0), forward[...], preferred_element_type=jnp.float32
+        ).reshape(2 * block, few, 2 * nr)
+        estimated[records] = result[:block]
+        observed[records] = result[block:]
+
+    def to_estimate(start, shots):
         results = []
         for parity in range(2):
             start_lane = 2 * nr * parity
             both = x[pl.ds(start, shots), :, start_lane : start_lane + 2 * nr]
             both = both.reshape(shots * few, 2 * nr)
             rows = jnp.concatenate([both, both[:, :nr]], axis=1)
-            result = jnp.dot(rows, table[parity], preferred_element_type=jnp.float32)
+            result = jnp.dot(rows, inverse[parity], preferred_element_type=jnp.float32)
             results.append(result.reshape(shots, few, nr))
-        return results
-
-    def to_lines(pair, pairs):
-        for parity, result in enumerate(receivers(pair * span, pairs * span, forward)):
-            lanes = slice(parity * nr, (parity + 1) * nr)
-            for p in range(pairs):
-                for side in range(2):
-                    at = (2 * p + side) * block
-                    target = pl.ds((pair + p + side * half) * block, block)
-                    lines[target, :, lanes] = result[at : at + block]
-
-    def to_estimate(start, shots):
-        even, odd = receivers(start, shots, inverse)
+        even, odd = results
         for lanes, result in ((slice(0, hr), even + odd), (slice(hr, nr), even - odd)):
             for part in range(2):
                 e_all[part, pl.ds(start, shots), :, lanes] = result[
@@ -479,10 +470,10 @@
         column_sums = jnp.sum(jnp.where(diagonal, whole, 0.0), axis=1, keepdims=True)
         limit[...] = jnp.broadcast_to(column_sums, (n, LANES))
 
-    scale = 1.0 / (span * nr)
     count = span * few * n * nf * nr
 
-    def synthesise(j, carried):
+    def synthesise(last, j, carried):
+        scale = 1.0 / (span * nr) if last else 1.0 / span
         level = levels_ref[j].astype(jnp.float32) * (level_scale * scale / count)
         bound = limit[pl.ds(j, 1), :] * level
         for parity, c in columns:
@@ -499,7 +490,10 @@
                     lanes = slice(part * hr + c, part * hr + c + LANES)
                     if t < block:
                         value = parts[part] + carry[t, :, lanes]
-                        keep(j * block + t, parity, part * hr + c - parity * nr, value)
+                        if last:
+                            keep(j * block + t, parity, part * hr + c - parity * nr, value)
+                        else:
+                            estimated[j * block + t, :, lanes] = value
                     else:
                         carry[t - block, :, lanes] = parts[part]
         return carried
@@ -507,22 +501,17 @@
     for step in range(PASSES):
         if step == 0:
             for near in range(half):
-                for copy in record_copies[near] + record_copies[near + half]:
-                    copy.wait()
-                pair = peers[near] % half
-                relax(pair, 0)
-                to_lines(pair, 1)
+                for k in (near, near + half):
+                    for copy in record_copies[k]:
+                        copy.wait()
+                    to_lines(peers[k])
+                relax(peers[near] % half, 0)
         else:
             lax.fori_loop(0, half, relax, 0)
-            for pair in range(0, half, half // 2):
-                to_lines(pair, half // 2)
         analyse(step)
         thresholds(step)
         carry[...] = jnp.zeros_like(carry)
-        lax.fori_loop(0, n, synthesise, 0)
-        if step < PASSES - 1:
-            for start in (0, total // 2):
-                to_estimate(start, total // 2)
+        lax.fori_loop(0, n, functools.partial(synthesise, step == PASSES - 1), 0)
 
     copies = []
     for group in [(k, k + 1) for k in range(half, n, 2)] + [(2, 3), (0, 1)]:
@@ -555,15 +544,15 @@
     block, freq_local, nr = estimate.shape[1:]
     few = freq_local // n
     total = n * block
-    tables_both = fourier_matrices(nr)
+    forward, inverse = fourier_matrices(nr)
     f32, bf16 = jnp.float32, jnp.bfloat16
-    in_hbm = pl.BlockSpec(memory_space=pltpu.HBM)
+    anywhere = pl.BlockSpec(memory_space=pl.ANY)
     dma = pltpu.SemaphoreType.DMA
     return pl.pallas_call(
         functools.partial(deblend_kernel, n, nf, block, few, nr),
         out_shape=jax.ShapeDtypeStruct(estimate.shape, estimate.dtype),
-        in_specs=[in_hbm] * 6,
-        out_specs=pl.BlockSpec(memory_space=pl.ANY),
+        in_specs=[anywhere] * 7,
+        out_specs=anywhere,
         scratch_shapes=[
             pltpu.SMEM(partner.shape, jnp.int32),
             pltpu.SMEM(delays.shape, jnp.int32),
@@ -573,17 +562,21 @@
             pltpu.VMEM((n, 8, LANES), jnp.int32),
             pltpu.VMEM((total, few, LANES), f32),
             pltpu.VMEM((total, few, LANES), f32),
-            pltpu.VMEM((total, few, LANES), jnp.int32),
+            pltpu.VMEM((8, LANES), jnp.int32),
+            pltpu.SMEM((8, LANES), jnp.int32),
             pltpu.VMEM((total, few, 4 * nr), bf16),
+            pltpu.VMEM((total, few, 2 * nr), f32),
+            pltpu.VMEM((total, few, 2 * nr), f32),
             pltpu.VMEM((total + block, few, 2 * nr), f32),
             pltpu.VMEM((n, 2 * block, few, 2 * nr), f32),
             pltpu.VMEM((block, few, 2 * nr), f32),
             pltpu.VMEM((n, LANES), f32),
             pltpu.VMEM((PASSES, n * nf, 1, LANES), f32),
-            pltpu.VMEM(tables_both.shape, f32),
+            pltpu.VMEM(forward.shape, f32),
+            pltpu.VMEM(inverse.shape, f32),
+            pltpu.VMEM((4 * nr, 2 * nr), bf16),
             pltpu.VMEM((2, 3 * nr, nr), bf16),
-            pltpu.VMEM((2, 3 * nr, nr), bf16),
-            dma((6,)),
+            dma((8,)),
             dma((n,)),
             dma((n,)),
             dma((n,)),
@@ -596,9 +589,9 @@
             dma((n,)),
         ],
         compiler_params=pltpu.CompilerParams(
-            collective_id=0, has_side_effects=True, vmem_limit_bytes=40 * 1024 * 1024
+            collective_id=0, has_side_effects=True, vmem_limit_bytes=60 * 1024 * 1024
         ),
-    )(blended, estimate, partner, delays, levels, jnp.asarray(tables_both))
+    )(blended, estimate, partner, delays, levels, jnp.asarray(forward), jnp.asarray(inverse))
 
 
 def solution(mesh):

time: 65 us -> 58.9 us (0.906)
  local copies, waits for them, and re-layouts: 6.07 us -> 1.87 us
  Pallas kernels: 58.6 us -> 56.9 us
    unnamed x13 -> x1, local copies, waits for them, and re-layouts: 6.07 us -> 1.87 us
    pallas_call x1, Pallas kernels: 58.6 us -> 56.9 us  [in_one_kernel(): pl.pallas_call(functools.partial(deblend_kernel, n, nf, block, few, nr),...]
where the time goes in v4:
time: 58.9 us; the launch traced here: 58.8 us
  Pallas kernels  56.9 us (97%)
  local copies, waits for them, and re-layouts  1.87 us (3%)
    pallas_call x1, Pallas kernels, in_one_kernel(): pl.pallas_call(functools.partial(deblend_kernel, n, nf, block, few, nr),...  56.9 us
    unnamed x1, local copies, waits for them, and re-layouts  1.87 us

profile of v4, /device:TPU:0, one launch (start us, length us, event | category | flops | bytes accessed | tf_op | source)
XLA Modules:
  0.0 58.8 jit_solution(9905501100870371785)
XLA Ops:
  0.0 56.9 %shard_map.73 = bf16[2,4,128,256]{3,2,1,0:T(8,128)(2,1)} custom-call(bf16[2,4,128,256]{3,2,1,0:T(8,128)(2,1)} %blended_ref.1, bf16[2,4,128,256]{3,2,1,0:T(8,128)(2,1)} %estimate_ref.1, s32[4]{0:T(128)} %partner_hbm.1, s32[32]{0:T(128)} %delays_hbm.1, s32[8]{0:T(128)} %levels_hbm.1, f32[512,512]{1,0:T(8,128)} %constant.4.clone.forward_hbm, ...), custom_call_target="tpu_custom_call" | custom-call | tf_op jit(solution)/shard_map/pallas_call | solution.py:551
  56.9 1.9 %copy.9 = bf16[2,4,128,256]{3,2,1,0:T(8,128)(2,1)} copy(bf16[2,4,128,256]{3,2,1,0:T(8,128)(2,1)} %shard_map.73) | data formatting | bytes 1048576

commit v5 on v4

--- a/solution.py
+++ b/solution.py
@@ -211,6 +211,8 @@
     partner_ref,
     delays_ref,
     levels_ref,
+    e_home,
+    b_home,
     e_all,
     b_all,
     info,
@@ -267,6 +269,12 @@
     ]
     for copy in scalar_copies:
         copy.start()
+    home_copies = [
+        pltpu.make_async_copy(estimate_ref, e_home, local_sem.at[8]),
+        pltpu.make_async_copy(blended_ref, b_home, local_sem.at[9]),
+    ]
+    for copy in home_copies:
+        copy.start()
     local_copies = [
         pltpu.make_async_copy(forward_hbm, exact_forward, local_sem.at[0]),
         pltpu.make_async_copy(inverse_hbm, exact_inverse, local_sem.at[6]),
@@ -297,6 +305,8 @@
         tile = jnp.where(here & (row == 0), mate, tile)
         tile = jnp.where(here & (row == 1), offset, tile)
     info[0] = tile
+    for copy in home_copies:
+        copy.wait()
 
     pl.semaphore_wait(barrier, n * nf - 1)
 
@@ -320,8 +330,8 @@
     record_copies[0] = local_copies[2:]
     for k in order:
         for held, whole, sent, received in (
-            (estimate_ref, e_all, e_send, e_recv),
-            (blended_ref, b_all, b_send, b_recv),
+            (e_home, e_all, e_send, e_recv),
+            (b_home, b_all, b_send, b_recv),
         ):
             record_copies[k].append(
                 send(
@@ -472,7 +482,7 @@
 
     count = span * few * n * nf * nr
 
-    def synthesise(last, j, carried):
+    def synthesise(last, j, carried, firsts=True):
         scale = 1.0 / (span * nr) if last else 1.0 / span
         level = levels_ref[j].astype(jnp.float32) * (level_scale * scale / count)
         bound = limit[pl.ds(j, 1), :] * level
@@ -488,6 +498,8 @@
             for t, parts in enumerate(short_fourier(values, 1)):
                 for part in range(2):
                     lanes = slice(part * hr + c, part * hr + c + LANES)
+                    if t < block and not firsts:
+                        continue
                     if t < block:
                         value = parts[part] + carry[t, :, lanes]
                         if last:
@@ -510,12 +522,25 @@
             lax.fori_loop(0, half, relax, 0)
         analyse(step)
         thresholds(step)
-        carry[...] = jnp.zeros_like(carry)
-        lax.fori_loop(0, n, functools.partial(synthesise, step == PASSES - 1), 0)
+        if step < PASSES - 1:
+            carry[...] = jnp.zeros_like(carry)
+            lax.fori_loop(0, n, functools.partial(synthesise, False), 0)
 
     copies = []
     for group in [(k, k + 1) for k in range(half, n, 2)] + [(2, 3), (0, 1)]:
-        to_estimate(peers[group[0]] // 2 * 2 * block, 2 * block)
+        first = peers[group[0]] // 2 * 2
+
+        @pl.when(first == 0)
+        def _():
+            carry[...] = jnp.zeros_like(carry)
+
+        @pl.when(first > 0)
+        def _():
+            synthesise(True, first - 1, 0, firsts=False)
+
+        synthesise(True, first, 0)
+        synthesise(True, first + 1, 0)
+        to_estimate(first * block, 2 * block)
         for k in group:
             if k:
                 copies.append(
@@ -540,6 +565,20 @@
     last.wait()
 
 
+def copy_kernel(source_ref, target_ref, sems):
+    copies = [
+        pltpu.make_async_copy(
+            source_ref.at[part, i], target_ref.at[part, i], sems.at[part, i]
+        )
+        for part in range(source_ref.shape[0])
+        for i in range(source_ref.shape[1])
+    ]
+    for copy in copies:
+        copy.start()
+    for copy in copies:
+        copy.wait()
+
+
 def in_one_kernel(n, nf, blended, estimate, partner, delays, levels):
     block, freq_local, nr = estimate.shape[1:]
     few = freq_local // n
@@ -548,7 +587,7 @@
     f32, bf16 = jnp.float32, jnp.bfloat16
     anywhere = pl.BlockSpec(memory_space=pl.ANY)
     dma = pltpu.SemaphoreType.DMA
-    return pl.pallas_call(
+    result = pl.pallas_call(
         functools.partial(deblend_kernel, n, nf, block, few, nr),
         out_shape=jax.ShapeDtypeStruct(estimate.shape, estimate.dtype),
         in_specs=[anywhere] * 7,
@@ -557,6 +596,8 @@
             pltpu.SMEM(partner.shape, jnp.int32),
             pltpu.SMEM(delays.shape, jnp.int32),
             pltpu.SMEM(levels.shape, jnp.int32),
+            pltpu.VMEM(estimate.shape, bf16),
+            pltpu.VMEM(blended.shape, bf16),
             pltpu.VMEM((2, total, few, nr), bf16),
             pltpu.VMEM((2, total, few, nr), bf16),
             pltpu.VMEM((n, 8, LANES), jnp.int32),
@@ -576,7 +617,7 @@
             pltpu.VMEM(inverse.shape, f32),
             pltpu.VMEM((4 * nr, 2 * nr), bf16),
             pltpu.VMEM((2, 3 * nr, nr), bf16),
-            dma((8,)),
+            dma((10,)),
             dma((n,)),
             dma((n,)),
             dma((n,)),
@@ -592,6 +633,14 @@
             collective_id=0, has_side_effects=True, vmem_limit_bytes=60 * 1024 * 1024
         ),
     )(blended, estimate, partner, delays, levels, jnp.asarray(forward), jnp.asarray(inverse))
+    return pl.pallas_call(
+        copy_kernel,
+        out_shape=jax.ShapeDtypeStruct(estimate.shape, estimate.dtype),
+        in_specs=[anywhere],
+        out_specs=anywhere,
+        scratch_shapes=[dma(estimate.shape[:2])],
+        compiler_params=pltpu.CompilerParams(vmem_limit_bytes=60 * 1024 * 1024),
+    )(result)
 
 
 def solution(mesh):

time: 58.9 us -> 73.4 us (1.25)
  Pallas kernels: 56.9 us -> 73.3 us
  local copies, waits for them, and re-layouts: 1.87 us -> 0 us
    pallas_call x0 -> x1, Pallas kernels: none -> 17.1 us  [in_one_kernel(): pl.pallas_call(copy_kernel, out_shape=jax.ShapeDtypeStruct(estimate.shape...]
    unnamed x1 -> x0, local copies, waits for them, and re-layouts: 1.87 us -> none
where the time goes in v5:
time: 73.4 us; the launch traced here: 73.3 us
  Pallas kernels  73.3 us (100%)
    pallas_call x1, Pallas kernels, in_one_kernel(): pl.pallas_call(functools.partial(deblend_kernel, n, nf, block, few, nr),...  56.2 us
    pallas_call x1, Pallas kernels, in_one_kernel(): pl.pallas_call(copy_kernel, out_shape=jax.ShapeDtypeStruct(estimate.shape...  17.1 us

profile of v5, /device:TPU:0, one launch (start us, length us, event | category | flops | bytes accessed | tf_op | source)
XLA Modules:
  0.0 73.3 jit_solution(5354030188919190446)
XLA Ops:
  0.0 56.2 %shard_map.73.source_ref = bf16[2,4,128,256]{3,2,1,0:T(8,128)(2,1)} custom-call(bf16[2,4,128,256]{3,2,1,0:T(8,128)(2,1)} %blended_ref.1, bf16[2,4,128,256]{3,2,1,0:T(8,128)(2,1)} %estimate_ref.1, s32[4]{0:T(128)} %partner_hbm.1, s32[32]{0:T(128)} %delays_hbm.1, s32[8]{0:T(128)} %levels_hbm.1, f32[512,512]{1,0:T(8,128)} %constant.4.clone.forward_hbm, ...), custom_call_target="tpu_custom_call" | custom-call | tf_op jit(solution)/shard_map/pallas_call | solution.py:590
  56.2 17.1 %shard_map.74 = bf16[2,4,128,256]{3,2,1,0:T(8,128)(2,1)} custom-call(bf16[2,4,128,256]{3,2,1,0:T(8,128)(2,1)} %shard_map.73.source_ref), custom_call_target="tpu_custom_call" | custom-call | tf_op jit(solution)/shard_map/pallas_call | solution.py:636

commit v6 on v5

--- a/solution.py
+++ b/solution.py
@@ -253,7 +253,7 @@
     column = lax.axis_index("freq")
     mesh_id = pl.DeviceIdType.MESH
     peers = [flipped(me, k, n) for k in range(n)]
-    order = [half] + [k for near in range(1, half) for k in (near + half, near)]
+    order = list(range(half, n)) + list(range(1, half))
     others = [lax.rem(column + k, nf) for k in range(nf)]
     everyone = [(k, f) for k in order + [0] for f in range(nf) if (k, f) != (0, 0)]
 
@@ -345,7 +345,7 @@
 
     lines[pl.ds(total, block)] = jnp.zeros((block, few, 2 * nr), jnp.float32)
     for copy in info_copies:
-        copy.wait()
+        copy.wait_recv()
     known = info[0]
     for k in range(1, n):
         known = known + info[k]
@@ -449,7 +449,7 @@
 
         lax.fori_loop(0, n, window, 0)
 
-    departures = []
+    departures = list(info_copies)
     diagonal = lax.broadcasted_iota(jnp.int32, (n, LANES), 0) == lax.broadcasted_iota(
         jnp.int32, (n, LANES), 1
     )
@@ -515,7 +515,11 @@
             for near in range(half):
                 for k in (near, near + half):
                     for copy in record_copies[k]:
-                        copy.wait()
+                        if k:
+                            copy.wait_recv()
+                            departures.append(copy)
+                        else:
+                            copy.wait()
                     to_lines(peers[k])
                 relax(peers[near] % half, 0)
         else:
@@ -565,17 +569,20 @@
     last.wait()
 
 
-def copy_kernel(source_ref, target_ref, sems):
-    copies = [
-        pltpu.make_async_copy(
-            source_ref.at[part, i], target_ref.at[part, i], sems.at[part, i]
-        )
-        for part in range(source_ref.shape[0])
-        for i in range(source_ref.shape[1])
+def copy_kernel(source_ref, target_ref, held, in_sems, out_sems):
+    pieces = [(part, i) for part in range(source_ref.shape[0]) for i in range(source_ref.shape[1])]
+    arrivals = [
+        pltpu.make_async_copy(source_ref.at[at], held.at[at], in_sems.at[at]) for at in pieces
     ]
-    for copy in copies:
+    departures = [
+        pltpu.make_async_copy(held.at[at], target_ref.at[at], out_sems.at[at]) for at in pieces
+    ]
+    for copy in arrivals:
         copy.start()
-    for copy in copies:
+    for arrival, departure in zip(arrivals, departures):
+        arrival.wait()
+        departure.start()
+    for copy in departures:
         copy.wait()
 
 
@@ -638,7 +645,11 @@
         out_shape=jax.ShapeDtypeStruct(estimate.shape, estimate.dtype),
         in_specs=[anywhere],
         out_specs=anywhere,
-        scratch_shapes=[dma(estimate.shape[:2])],
+        scratch_shapes=[
+            pltpu.VMEM(estimate.shape, bf16),
+            dma(estimate.shape[:2]),
+            dma(estimate.shape[:2]),
+        ],
         compiler_params=pltpu.CompilerParams(vmem_limit_bytes=60 * 1024 * 1024),
     )(result)
 

time: 73.4 us -> 58.3 us (0.79)
  Pallas kernels: 73.3 us -> 58.1 us
    pallas_call x1, Pallas kernels: 17.1 us -> 1.83 us  [in_one_kernel(): pl.pallas_call(copy_kernel, out_shape=jax.ShapeDtypeStruct(estimate.shape...]
where the time goes in v6:
time: 58.3 us; the launch traced here: 58.1 us
  Pallas kernels  58.1 us (100%)
    pallas_call x1, Pallas kernels, in_one_kernel(): pl.pallas_call(functools.partial(deblend_kernel, n, nf, block, few, nr),...  56.3 us
    pallas_call x1, Pallas kernels, in_one_kernel(): pl.pallas_call(copy_kernel, out_shape=jax.ShapeDtypeStruct(estimate.shape...  1.83 us

profile of v6, /device:TPU:0, one launch (start us, length us, event | category | flops | bytes accessed | tf_op | source)
XLA Modules:
  0.0 58.1 jit_solution(17074357774501937124)
XLA Ops:
  0.0 56.3 %shard_map.73.source_ref = bf16[2,4,128,256]{3,2,1,0:T(8,128)(2,1)} custom-call(bf16[2,4,128,256]{3,2,1,0:T(8,128)(2,1)} %blended_ref.1, bf16[2,4,128,256]{3,2,1,0:T(8,128)(2,1)} %estimate_ref.1, s32[4]{0:T(128)} %partner_hbm.1, s32[32]{0:T(128)} %delays_hbm.1, s32[8]{0:T(128)} %levels_hbm.1, f32[512,512]{1,0:T(8,128)} %constant.4.clone.forward_hbm, ...), custom_call_target="tpu_custom_call" | custom-call | tf_op jit(solution)/shard_map/pallas_call | solution.py:597
  56.3 1.8 %shard_map.74 = bf16[2,4,128,256]{3,2,1,0:T(8,128)(2,1)} custom-call(bf16[2,4,128,256]{3,2,1,0:T(8,128)(2,1)} %shard_map.73.source_ref), custom_call_target="tpu_custom_call" | custom-call | tf_op jit(solution)/shard_map/pallas_call | solution.py:643

commit v7 on v6

--- a/solution.py
+++ b/solution.py
@@ -257,10 +257,17 @@
     others = [lax.rem(column + k, nf) for k in range(nf)]
     everyone = [(k, f) for k in order + [0] for f in range(nf) if (k, f) != (0, 0)]
 
+    second = n - n // 4
+    am_second = me >= second
+    same = [(peers[k] >= second) == am_second for k in range(n)]
     barrier = pltpu.get_barrier_semaphore()
-    for k, f in everyone:
-        where = {"shot": peers[k], "freq": others[f]}
-        pl.semaphore_signal(barrier, inc=1, device_id=where, device_id_type=mesh_id)
+
+    def greet(k):
+        for f in range(nf):
+            if (k, f) != (0, 0):
+                where = {"shot": peers[k], "freq": others[f]}
+                pl.semaphore_signal(barrier, inc=1, device_id=where, device_id_type=mesh_id)
+
 
     scalar_copies = [
         pltpu.make_async_copy(partner_hbm, partner_ref, local_sem.at[3]),
@@ -292,6 +299,10 @@
     for copy in local_copies:
         copy.start()
 
+    greet(0)
+    for k in order:
+        pl.when(same[k])(functools.partial(greet, k))
+
     for copy in scalar_copies:
         copy.wait()
     lane = lax.broadcasted_iota(jnp.int32, (8, LANES), 1)
@@ -308,9 +319,11 @@
     for copy in home_copies:
         copy.wait()
 
-    pl.semaphore_wait(barrier, n * nf - 1)
-
-    def send(source, target, send_sem, recv_sem, where):
+    pl.semaphore_wait(barrier, jnp.where(am_second, n * nf - 1, second * nf - 1))
+    for k in order:
+        pl.when(jnp.logical_not(same[k]))(functools.partial(greet, k))
+
+    def send(source, target, send_sem, recv_sem, where, start=True):
         copy = pltpu.make_async_remote_copy(
             src_ref=source,
             dst_ref=target,
@@ -319,16 +332,18 @@
             device_id=where,
             device_id_type=mesh_id,
         )
-        copy.start()
+        if start:
+            copy.start()
         return copy
 
-    info_copies = [
-        send(info.at[0], info.at[k], info_send.at[k], info_recv.at[k], {"shot": peers[k]})
-        for k in order
-    ]
     record_copies = {k: [] for k in range(n)}
     record_copies[0] = local_copies[2:]
+    info_copies = []
     for k in order:
+        where = {"shot": peers[k]}
+        info_copies.append(
+            send(info.at[0], info.at[k], info_send.at[k], info_recv.at[k], where, start=False)
+        )
         for held, whole, sent, received in (
             (e_home, e_all, e_send, e_recv),
             (b_home, b_all, b_send, b_recv),
@@ -339,9 +354,26 @@
                     whole.at[:, pl.ds(me * block, block)],
                     sent.at[k],
                     received.at[k],
-                    {"shot": peers[k]},
+                    where,
+                    start=False,
                 )
             )
+
+    def begin(k, info_copy):
+        info_copy.start()
+        for copy in record_copies[k]:
+            copy.start()
+
+    for k, info_copy in zip(order, info_copies):
+        pl.when(jnp.logical_or(am_second, same[k]))(functools.partial(begin, k, info_copy))
+
+    @pl.when(jnp.logical_not(am_second))
+    def _():
+        pl.semaphore_wait(barrier, (n - second) * nf)
+
+    for k, info_copy in zip(order, info_copies):
+        late = jnp.logical_not(jnp.logical_or(am_second, same[k]))
+        pl.when(late)(functools.partial(begin, k, info_copy))
 
     lines[pl.ds(total, block)] = jnp.zeros((block, few, 2 * nr), jnp.float32)
     for copy in info_copies:
@@ -569,23 +601,6 @@
     last.wait()
 
 
-def copy_kernel(source_ref, target_ref, held, in_sems, out_sems):
-    pieces = [(part, i) for part in range(source_ref.shape[0]) for i in range(source_ref.shape[1])]
-    arrivals = [
-        pltpu.make_async_copy(source_ref.at[at], held.at[at], in_sems.at[at]) for at in pieces
-    ]
-    departures = [
-        pltpu.make_async_copy(held.at[at], target_ref.at[at], out_sems.at[at]) for at in pieces
-    ]
-    for copy in arrivals:
-        copy.start()
-    for arrival, departure in zip(arrivals, departures):
-        arrival.wait()
-        departure.start()
-    for copy in departures:
-        copy.wait()
-
-
 def in_one_kernel(n, nf, blended, estimate, partner, delays, levels):
     block, freq_local, nr = estimate.shape[1:]
     few = freq_local // n
@@ -594,7 +609,7 @@
     f32, bf16 = jnp.float32, jnp.bfloat16
     anywhere = pl.BlockSpec(memory_space=pl.ANY)
     dma = pltpu.SemaphoreType.DMA
-    result = pl.pallas_call(
+    return pl.pallas_call(
         functools.partial(deblend_kernel, n, nf, block, few, nr),
         out_shape=jax.ShapeDtypeStruct(estimate.shape, estimate.dtype),
         in_specs=[anywhere] * 7,
@@ -640,18 +655,6 @@
             collective_id=0, has_side_effects=True, vmem_limit_bytes=60 * 1024 * 1024
         ),
     )(blended, estimate, partner, delays, levels, jnp.asarray(forward), jnp.asarray(inverse))
-    return pl.pallas_call(
-        copy_kernel,
-        out_shape=jax.ShapeDtypeStruct(estimate.shape, estimate.dtype),
-        in_specs=[anywhere],
-        out_specs=anywhere,
-        scratch_shapes=[
-            pltpu.VMEM(estimate.shape, bf16),
-            dma(estimate.shape[:2]),
-            dma(estimate.shape[:2]),
-        ],
-        compiler_params=pltpu.CompilerParams(vmem_limit_bytes=60 * 1024 * 1024),
-    )(result)
 
 
 def solution(mesh):

time: 58.3 us -> 59.7 us (1.024)
  local copies, waits for them, and re-layouts: 0 us -> 1.87 us
    unnamed x0 -> x1, local copies, waits for them, and re-layouts: none -> 1.87 us
    pallas_call x1 -> x0, Pallas kernels: 1.83 us -> none  [in_one_kernel(): pl.pallas_call(copy_kernel, out_shape=jax.ShapeDtypeStruct(estimate.shape...]
    pallas_call x1, Pallas kernels: 56.3 us -> 57.6 us  [in_one_kernel(): pl.pallas_call(functools.partial(deblend_kernel, n, nf, block, few, nr),...]
where the time goes in v7:
time: 59.7 us; the launch traced here: 59.5 us
  Pallas kernels  57.6 us (96%)
  local copies, waits for them, and re-layouts  1.87 us (3%)
    pallas_call x1, Pallas kernels, in_one_kernel(): pl.pallas_call(functools.partial(deblend_kernel, n, nf, block, few, nr),...  57.6 us
    unnamed x1, local copies, waits for them, and re-layouts  1.87 us

profile of v7, /device:TPU:0, one launch (start us, length us, event | category | flops | bytes accessed | tf_op | source)
XLA Modules:
  0.0 59.5 jit_solution(9330049651560193659)
XLA Ops:
  0.0 57.6 %shard_map.73 = bf16[2,4,128,256]{3,2,1,0:T(8,128)(2,1)} custom-call(bf16[2,4,128,256]{3,2,1,0:T(8,128)(2,1)} %blended_ref.1, bf16[2,4,128,256]{3,2,1,0:T(8,128)(2,1)} %estimate_ref.1, s32[4]{0:T(128)} %partner_hbm.1, s32[32]{0:T(128)} %delays_hbm.1, s32[8]{0:T(128)} %levels_hbm.1, f32[512,512]{1,0:T(8,128)} %constant.4.clone.forward_hbm, ...), custom_call_target="tpu_custom_call" | custom-call | tf_op jit(solution)/shard_map/pallas_call | solution.py:612
  57.6 1.9 %copy.9 = bf16[2,4,128,256]{3,2,1,0:T(8,128)(2,1)} copy(bf16[2,4,128,256]{3,2,1,0:T(8,128)(2,1)} %shard_map.73) | data formatting | bytes 1048576

commit v8 on v6

--- a/solution.py
+++ b/solution.py
@@ -255,12 +255,9 @@
     peers = [flipped(me, k, n) for k in range(n)]
     order = list(range(half, n)) + list(range(1, half))
     others = [lax.rem(column + k, nf) for k in range(nf)]
-    everyone = [(k, f) for k in order + [0] for f in range(nf) if (k, f) != (0, 0)]
+    everyone = [(k, f) for k in reversed(range(n)) for f in range(nf) if (k, f) != (0, 0)]
 
     barrier = pltpu.get_barrier_semaphore()
-    for k, f in everyone:
-        where = {"shot": peers[k], "freq": others[f]}
-        pl.semaphore_signal(barrier, inc=1, device_id=where, device_id_type=mesh_id)
 
     scalar_copies = [
         pltpu.make_async_copy(partner_hbm, partner_ref, local_sem.at[3]),
@@ -292,6 +289,9 @@
     for copy in local_copies:
         copy.start()
 
+    for k, f in everyone:
+        where = {"shot": peers[k], "freq": others[f]}
+        pl.semaphore_signal(barrier, inc=1, device_id=where, device_id_type=mesh_id)
     for copy in scalar_copies:
         copy.wait()
     lane = lax.broadcasted_iota(jnp.int32, (8, LANES), 1)
@@ -569,23 +569,6 @@
     last.wait()
 
 
-def copy_kernel(source_ref, target_ref, held, in_sems, out_sems):
-    pieces = [(part, i) for part in range(source_ref.shape[0]) for i in range(source_ref.shape[1])]
-    arrivals = [
-        pltpu.make_async_copy(source_ref.at[at], held.at[at], in_sems.at[at]) for at in pieces
-    ]
-    departures = [
-        pltpu.make_async_copy(held.at[at], target_ref.at[at], out_sems.at[at]) for at in pieces
-    ]
-    for copy in arrivals:
-        copy.start()
-    for arrival, departure in zip(arrivals, departures):
-        arrival.wait()
-        departure.start()
-    for copy in departures:
-        copy.wait()
-
-
 def in_one_kernel(n, nf, blended, estimate, partner, delays, levels):
     block, freq_local, nr = estimate.shape[1:]
     few = freq_local // n
@@ -594,7 +577,7 @@
     f32, bf16 = jnp.float32, jnp.bfloat16
     anywhere = pl.BlockSpec(memory_space=pl.ANY)
     dma = pltpu.SemaphoreType.DMA
-    result = pl.pallas_call(
+    return pl.pallas_call(
         functools.partial(deblend_kernel, n, nf, block, few, nr),
         out_shape=jax.ShapeDtypeStruct(estimate.shape, estimate.dtype),
         in_specs=[anywhere] * 7,
@@ -640,18 +623,6 @@
             collective_id=0, has_side_effects=True, vmem_limit_bytes=60 * 1024 * 1024
         ),
     )(blended, estimate, partner, delays, levels, jnp.asarray(forward), jnp.asarray(inverse))
-    return pl.pallas_call(
-        copy_kernel,
-        out_shape=jax.ShapeDtypeStruct(estimate.shape, estimate.dtype),
-        in_specs=[anywhere],
-        out_specs=anywhere,
-        scratch_shapes=[
-            pltpu.VMEM(estimate.shape, bf16),
-            dma(estimate.shape[:2]),
-            dma(estimate.shape[:2]),
-        ],
-        compiler_params=pltpu.CompilerParams(vmem_limit_bytes=60 * 1024 * 1024),
-    )(result)
 
 
 def solution(mesh):

time: 58.3 us -> 58.4 us (level)
  local copies, waits for them, and re-layouts: 0 us -> 1.87 us
  Pallas kernels: 58.1 us -> 56.3 us
    unnamed x0 -> x1, local copies, waits for them, and re-layouts: none -> 1.87 us
    pallas_call x1 -> x0, Pallas kernels: 1.83 us -> none  [in_one_kernel(): pl.pallas_call(copy_kernel, out_shape=jax.ShapeDtypeStruct(estimate.shape...]
where the time goes in v8:
time: 58.4 us; the launch traced here: 58.2 us
  Pallas kernels  56.3 us (96%)
  local copies, waits for them, and re-layouts  1.87 us (3%)
    pallas_call x1, Pallas kernels, in_one_kernel(): pl.pallas_call(functools.partial(deblend_kernel, n, nf, block, few, nr),...  56.3 us
    unnamed x1, local copies, waits for them, and re-layouts  1.87 us

profile of v8, /device:TPU:0, one launch (start us, length us, event | category | flops | bytes accessed | tf_op | source)
XLA Modules:
  0.0 58.2 jit_solution(18077521093116127064)
XLA Ops:
  0.0 56.3 %shard_map.73 = bf16[2,4,128,256]{3,2,1,0:T(8,128)(2,1)} custom-call(bf16[2,4,128,256]{3,2,1,0:T(8,128)(2,1)} %blended_ref.1, bf16[2,4,128,256]{3,2,1,0:T(8,128)(2,1)} %estimate_ref.1, s32[4]{0:T(128)} %partner_hbm.1, s32[32]{0:T(128)} %delays_hbm.1, s32[8]{0:T(128)} %levels_hbm.1, f32[512,512]{1,0:T(8,128)} %constant.4.clone.forward_hbm, ...), custom_call_target="tpu_custom_call" | custom-call | tf_op jit(solution)/shard_map/pallas_call | solution.py:580
  56.4 1.9 %copy.9 = bf16[2,4,128,256]{3,2,1,0:T(8,128)(2,1)} copy(bf16[2,4,128,256]{3,2,1,0:T(8,128)(2,1)} %shard_map.73) | data formatting | bytes 1048576
